TPU v7x, 32 devices: a whole 2x2x4 slice. The times are simulated.
32 devices in a mesh: dp: 8 (over z, x), expert: 4 (over y, core).
Axes of the slice: x: 2, y: 2, z: 4, core: 2. Of those that a mesh axis runs over, the one named last changes fastest.
Arguments:
- tokens: bfloat16 [4096, 1536], P(('dp', 'expert')), may hold values from -6 to 6
- cotangent: bfloat16 [4096, 1536], P(('dp', 'expert')), may hold values from -6 to 6
- routes: int32 [4096, 8], P(('dp', 'expert')), may hold values from 0 to 39, all different within a row; in each aligned block of 128 rows (0 to 127, 128 to 255, ...) at most 32 rows name the same one
- weight_qkv: float32 [1536, 2560], P(('dp', 'expert')), may hold values from -0.15625 to 0.15625
- moment_qkv: float32 [1536, 2560], P(('dp', 'expert')), may hold values from -128 to 128
- square_qkv: float32 [1536, 2560], P(('dp', 'expert')), may hold values from 1925.12 to 7782.4
- weight_out: float32 [1536, 1536], P(('dp', 'expert')), may hold values from -2.5 to 2.5
- moment_out: float32 [1536, 1536], P(('dp', 'expert')), may hold values from -5 to 5
- square_out: float32 [1536, 1536], P(('dp', 'expert')), may hold values from 0.53248 to 2.17088
- weight_router: float32 [1536, 40], P(('dp', 'expert')), may hold values from -0.078125 to 0.078125
- moment_router: float32 [1536, 40], P(('dp', 'expert')), may hold values from -128 to 128
- square_router: float32 [1536, 40], P(('dp', 'expert')), may hold values from 1925.12 to 7782.4
- gains: float32 [2, 1536], P(None, ('dp', 'expert')), may hold values from 0.5 to 1.5
- moment_gains: float32 [2, 1536], P(None, ('dp', 'expert')), may hold values from -80 to 80
- square_gains: float32 [2, 1536], P(None, ('dp', 'expert')), may hold values from 860.16 to 3440.64
- weight_gate_up: float32 [40, 1536, 1024], P('expert', 'dp'), may hold values from -0.15625 to 0.15625
- moment_gate_up: float32 [40, 1536, 1024], P('expert', 'dp'), may hold values from -6 to 6
- square_gate_up: float32 [40, 1536, 1024], P('expert', 'dp'), may hold values from 3.6864 to 14.7456
- weight_down: float32 [40, 512, 1536], P('expert', 'dp'), may hold values from -3 to 3
- moment_down: float32 [40, 512, 1536], P('expert', 'dp'), may hold values from -0.75 to 0.75
- square_down: float32 [40, 512, 1536], P('expert', 'dp'), may hold values from 0.0118784 to 0.0475136
Outputs:
- layer_out: bfloat16 [4096, 1536], P(('dp', 'expert'))
- token_grad: float32 [4096, 1536], P(('dp', 'expert'))
- new_weight_qkv: float32 [1536, 2560], P(('dp', 'expert'))
- new_moment_qkv: float32 [1536, 2560], P(('dp', 'expert'))
- new_square_qkv: float32 [1536, 2560], P(('dp', 'expert'))
- new_weight_out: float32 [1536, 1536], P(('dp', 'expert'))
- new_moment_out: float32 [1536, 1536], P(('dp', 'expert'))
- new_square_out: float32 [1536, 1536], P(('dp', 'expert'))
- new_weight_router: float32 [1536, 40], P(('dp', 'expert'))
- new_moment_router: float32 [1536, 40], P(('dp', 'expert'))
- new_square_router: float32 [1536, 40], P(('dp', 'expert'))
- new_gains: float32 [2, 1536], P(None, ('dp', 'expert'))
- new_moment_gains: float32 [2, 1536], P(None, ('dp', 'expert'))
- new_square_gains: float32 [2, 1536], P(None, ('dp', 'expert'))
- new_weight_gate_up: float32 [40, 1536, 1024], P('expert', 'dp')
- new_moment_gate_up: float32 [40, 1536, 1024], P('expert', 'dp')
- new_square_gate_up: float32 [40, 1536, 1024], P('expert', 'dp')
- new_weight_down: float32 [40, 512, 1536], P('expert', 'dp')
- new_moment_down: float32 [40, 512, 1536], P('expert', 'dp')
- new_square_down: float32 [40, 512, 1536], P('expert', 'dp')
Inputs may be any that keep to these rules, and one draw needn't show every extreme that they name: `routes`: each row names 8 different experts. Among the rows of one device, no expert is named by more than 32 rows, and in every draw some device has an expert named by exactly 32.
All inputs are finite; a program needn't handle non-finite values.
Results may differ from a plain program's by a relative error of at most 0.02.
Values may be sent and summed in bfloat16 or wider, within the bound.
No kernel may reach another device: no remote copies, remote signals or barrier semaphores. Data moves between devices by JAX's collectives and lax.ppermute only.
A program may use at most 320 MiB of HBM per device.

v0:
```python
import functools

import jax
import jax.numpy as jnp
import numpy as np
from jax import lax
from jax.experimental import pallas as pl
from jax.experimental.pallas import tpu as pltpu
from jax.sharding import Mesh, PartitionSpec as P

D = 1536
QUERY_HEADS = 24
KEY_VALUE_HEADS = 8
HEAD_SIZE = 64
FF = 512
EXPERTS = 40
TOPK = 8
STEP = 10
QKV = 2560
LANES = 128
HEADS_WIDTH = QUERY_HEADS * HEAD_SIZE
KEYS_WIDTH = KEY_VALUE_HEADS * HEAD_SIZE

norm_eps = 1e-06
residual_scale = 0.22
score_scale = 0.125
beta_one = 0.9
beta_two = 0.95
adam_eps = 1e-08
weight_decay = 0.1

f32 = jnp.float32
bf16 = jnp.bfloat16
ALL = ("z", "x", "y", "core")
PLANE = ("z", "x")
SAME_CORE = ("z", "x", "y")


def rotary_tables(sequence_length, size):
    half = size // 2
    places = jnp.arange(sequence_length).astype(f32)[:, None]
    inverse = 10000.0 ** (-jnp.arange(half).astype(f32) * 2.0 / size)
    angles = places * inverse[None, :]
    return (jnp.cos(angles)[:, None, :], jnp.sin(angles)[:, None, :])


def apply_rotation(values, cosine_lookup, sine_lookup):
    half = values.shape[-1] // 2
    first = values[..., :half]
    second = values[..., half:]
    return jnp.concatenate(
        [
            first * cosine_lookup - second * sine_lookup,
            second * cosine_lookup + first * sine_lookup,
        ],
        axis=-1,
    )


def attention_scores(query_rotated, key_rot, causal):
    scores = (
        jnp.einsum("skgd,tkd->kgst", query_rotated, key_rot, preferred_element_type=f32)
        * score_scale
    )
    return jnp.where(causal, scores, -1e30)


def norm_backward(grad_normed, values, factor, gain):
    scaled = grad_normed * gain
    grad_gain = jnp.sum(grad_normed * values * factor, axis=0)
    value_gradient = factor * scaled - values * factor * factor * factor * jnp.mean(
        scaled * values, axis=-1, keepdims=True
    )
    return (value_gradient, grad_gain)


def adam_step(weight, moment, square, grad, rate, decay):
    moment = beta_one * moment + (1.0 - beta_one) * grad
    square = beta_two * square + (1.0 - beta_two) * grad * grad
    fixed_one = moment / (1.0 - beta_one**STEP)
    fixed_two = square / (1.0 - beta_two**STEP)
    weight = weight - rate * (fixed_one / (jnp.sqrt(fixed_two) + adam_eps) + decay * weight)
    return (weight, moment, square)


def dot(a, b):
    return jnp.dot(a, b, preferred_element_type=f32)


def dot_nt(a, b):
    return lax.dot_general(a, b, (((1,), (1,)), ((), ())), preferred_element_type=f32)


def dot_tn(a, b):
    return lax.dot_general(a, b, (((0,), (0,)), ((), ())), preferred_element_type=f32)


def pad_lanes(values):
    extra = -values.shape[-1] % LANES
    return jnp.pad(values, ((0, 0), (0, extra)))


def swap_core(values):
    return lax.ppermute(values, "core", [(0, 1), (1, 0)])


def keep_kernel(*refs):
    pass


def ring_order(n):
    return [0] + list(range(1, n, 2)) + list(range(n - 2 + n % 2, 0, -2))


def home_table(n):
    order = ring_order(n)
    place = {chip: at for at, chip in enumerate(order)}
    return np.array([[order[(place[i] - s) % n] for s in range(n)] for i in range(n)], np.int32)


def make_shards(sizes):
    nz, nx, ny = sizes
    length = {"z": nz, "x": nx, "y": ny}
    planes = nz * nx
    per_group = EXPERTS // (2 * ny)
    whole = per_group // planes
    spare = per_group - whole * planes
    piece = FF // planes
    wide = whole * FF
    narrow = spare * piece
    narrow_pad = narrow + -narrow % LANES
    units = wide + narrow_pad

    rings = {axis: ring_order(n) for axis, n in length.items()}
    places = {axis: i for i, axis in enumerate(("z", "x", "y", "core"))}
    shape = (nz, nx, ny, 2)

    def pairs_of(axes, step):
        pairs = []
        for at in np.ndindex(*shape):
            axis = axes[at[3]]
            ring = rings[axis]
            to = list(at)
            to[places[axis]] = ring[(ring.index(at[places[axis]]) + step) % len(ring)]
            pairs.append(
                (int(np.ravel_multi_index(at, shape)), int(np.ravel_multi_index(to, shape)))
            )
        return pairs

    def move(values, axes, step):
        return lax.ppermute(values, ALL, pairs_of(axes, step))

    def row_order(core):
        found = {}
        for axis, n in length.items():
            here = jnp.arange(n)[:, None] == lax.axis_index(axis)
            found[axis] = jnp.sum(jnp.where(here, jnp.asarray(home_table(n)), 0), axis=0)
        x = jnp.where(core == 0, found["x"][None, :], found["x"][:, None])
        y = jnp.where(core == 0, found["y"][:, None], found["y"][None, :])
        chip = (found["z"] * nx + x[:, :, None]) * ny + y[:, :, None]
        block = (chip[..., None] * 2 + jnp.arange(2)).reshape(-1, 1)
        rows = D // block.shape[0]
        kept = (block * rows + jnp.arange(rows)[None, :]).reshape(1, D)
        return (jnp.arange(D)[:, None] == kept).astype(bf16)

    def add_low(a, b):
        return (a.astype(f32) + b.astype(f32)).astype(bf16)

    parts = ((0, "x", "y"), (1, "y", "x"))

    def line_of(own):
        line = [own]
        for _ in range(nz - 1):
            line.append(move(line[-1], "zz", 1))
        return line

    def gather_tokens(line, late):
        half = line[0].shape[0] // 2
        packs = [
            jnp.concatenate([b[part * half : (part + 1) * half] for b in line], axis=0)
            for part, _, _ in parts
        ]
        packs = [after(p, late) for p in packs]
        for level in (1, 2):
            grown = []
            for pack, names in zip(packs, parts):
                axis = names[level]
                steps = [pack]
                for _ in range(length[axis] - 1):
                    steps.append(move(steps[-1], axis * 2, 1))
                grown.append(jnp.concatenate(steps, axis=0))
            packs = grown
        return jnp.concatenate(packs, axis=0)

    def block_order():
        found = {}
        for axis, n in length.items():
            here = jnp.arange(n)[:, None] == lax.axis_index(axis)
            found[axis] = jnp.sum(jnp.where(here, jnp.asarray(home_table(n)), 0), axis=0)
        z = found["z"][None, None, :]
        blocks = []
        for part, second, third in parts:
            at = {second: found[second][None, :, None], third: found[third][:, None, None]}
            chip = (z * nx + at["x"]) * ny + at["y"]
            blocks.append((chip * 2 + part).reshape(-1))
        return jnp.concatenate(blocks)

    def copy_kernel(order_ref, *refs):
        out_ref = refs[-1]
        for i, ref in enumerate(refs[:-1]):
            out_ref[i] = ref[0]

    def permute_blocks(values, order):
        count, each = order.shape[0], 4
        rows, columns = values.shape[0] // count, values.shape[1]
        values = values.reshape(count, rows, columns)
        result = pl.pallas_call(
            copy_kernel,
            grid_spec=pltpu.PrefetchScalarGridSpec(
                num_scalar_prefetch=1,
                grid=(count // each,),
                in_specs=[
                    pl.BlockSpec(
                        (1, rows, columns), lambda i, order, j=j: (order[i * each + j], 0, 0)
                    )
                    for j in range(each)
                ],
                out_specs=pl.BlockSpec((each, rows, columns), lambda i, order: (i, 0, 0)),
            ),
            out_shape=jax.ShapeDtypeStruct((count, rows, columns), values.dtype),
            cost_estimate=pl.CostEstimate(flops=0, bytes_accessed=2**24, transcendentals=0),
            compiler_params=pltpu.CompilerParams(vmem_limit_bytes=32 * 2**20),
        )(order, *[values] * each)
        return result.reshape(count * rows, columns)

    def sum_level(packs, level):
        summed = []
        for pack, names in zip(packs, parts):
            n = length[names[level]]
            pack = pack.reshape(n, pack.shape[0] // n, *pack.shape[1:])
            acc = None
            for s in reversed(range(n)):
                acc = pack[s] if acc is None else add_low(move(acc, names[level] * 2, -1), pack[s])
            summed.append(acc)
        return summed

    def scatter_first(values):
        count = values.shape[0] // 2
        return sum_level([values[:count], values[count:]], 2)

    def scatter_second(halves):
        packs = [jnp.concatenate(same, axis=1) for same in zip(*halves)]
        packs = [p[0] for p in sum_level(packs, 1)]
        half = packs[0].shape[0] // nz
        return [
            jnp.concatenate([p[s * half : (s + 1) * half] for p in packs], axis=0)
            for s in range(nz)
        ]

    def sum_line(blocks):
        total = blocks[-1]
        for mine in reversed(blocks[:-1]):
            total = add_low(move(total, "zz", -1), mine)
        return total.astype(f32)

    def chip_half(own):
        half = own.shape[1] // 2
        core = lax.axis_index("core")
        left, right = own[:, :half], own[:, half:]
        kept = jnp.where(core == 0, left, right)
        came = swap_core(jnp.where(core == 0, right, left))
        return jnp.where(
            core == 0, jnp.concatenate([kept, came], axis=0), jnp.concatenate([came, kept], axis=0)
        )

    def gather_halves(line):
        rows, half = line[0].shape
        steps = [jnp.concatenate(line, axis=0)]
        for _ in range(nx - 1):
            steps.append(move(steps[-1], "xy", 1))
        packs = [jnp.concatenate(steps, axis=0)]
        for _ in range(nx - 1):
            packs.append(move(packs[-1], "yx", 1))
        result = jnp.concatenate(packs, axis=0)
        return result, swap_core(result)

    def scatter_halves_first(mine, other):
        both = add_low(swap_core(other), mine)
        grid = both.reshape(nx, nx, both.shape[0] // (nx * nx), both.shape[1])
        acc = None
        for s in reversed(range(nx)):
            acc = grid[s] if acc is None else add_low(move(acc, "yx", -1), grid[s])
        return acc

    def scatter_halves_second(acc, *late):
        core = lax.axis_index("core")
        rows = acc.shape[1] // (nz * 2)
        two = None
        for s in reversed(range(nx)):
            two = acc[s] if two is None else add_low(move(two, "xy", -1), acc[s])
        two = after(two, *late)
        total = None
        for s in reversed(range(nz)):
            mine = two[s * 2 * rows : (s + 1) * 2 * rows]
            total = mine if total is None else add_low(move(total, "zz", -1), mine)
        kept = jnp.where(core == 0, total[:rows], total[rows:])
        came = swap_core(jnp.where(core == 0, total[rows:], total[:rows]))
        return (
            jnp.where(core == 0, kept, came).astype(f32),
            jnp.where(core == 0, came, kept).astype(f32),
        )

    def after(values, *first, always=False):
        if not (whole or always):
            return values
        anywhere = pl.BlockSpec(memory_space=pl.ANY)
        return pl.pallas_call(
            keep_kernel,
            in_specs=[anywhere] * (1 + len(first)),
            out_specs=anywhere,
            out_shape=jax.ShapeDtypeStruct(values.shape, values.dtype),
            input_output_aliases={0: 0},
        )(values, *first)

    def all_to_all_plane(values):
        return lax.all_to_all(values, PLANE, split_axis=0, concat_axis=0, tiled=True)

    rows_home = D // planes
    across = rows_home // piece
    rest = 2 * narrow_pad + wide

    def cut_spare(part):
        part = part.reshape(spare, rows_home, 2, planes, piece)
        part = part.transpose(3, 1, 2, 0, 4).reshape(planes, rows_home, 2, narrow)
        part = jnp.pad(part, ((0, 0), (0, 0), (0, 0), (0, narrow_pad - narrow)))
        return part.reshape(planes, rows_home, 2 * narrow_pad)

    def join_spare(part):
        part = part.reshape(planes, rows_home, 2, narrow_pad)[..., :narrow]
        part = part.reshape(planes, rows_home, 2, spare, piece).transpose(3, 1, 2, 0, 4)
        return part.reshape(spare, rows_home, 2 * FF)

    def lanes(values, first, width=piece):
        return values[:, first : first + width]

    packed_columns = 2 * units + wide

    def pack_kernel(gate_up_ref, spare_ref, down_ref, spare_down_ref, out_ref, low_ref):
        step = pl.program_id(0)
        out_ref[step, :, pl.ds(0, 2 * wide)] = gate_up_ref[0].astype(bf16)
        for j in range(across):
            out_ref[step, pl.ds(j * piece, piece), pl.ds(2 * units, wide)] = down_ref[
                0, :, pl.ds(j * wide, wide)
            ].astype(bf16)

        @pl.when(step == 0)
        def _():
            for to in range(planes):
                taken = [
                    lanes(spare_ref[s], g * FF + to * piece) for g in range(2) for s in range(spare)
                ]
                out_ref[to, :, pl.ds(2 * wide, 2 * narrow)] = jnp.concatenate(taken, axis=1).astype(
                    bf16
                )
            for s in range(spare):
                low_ref[pl.ds(s * piece, piece), :] = spare_down_ref[s].astype(bf16)

    def pack_experts(gate_up, down):
        if not whole:
            low = down.astype(bf16).reshape(narrow, D)
            low = jnp.pad(low, ((0, narrow_pad - narrow), (0, 0)))
            return cut_spare(gate_up.astype(bf16)), low
        return pl.pallas_call(
            pack_kernel,
            grid=(planes,),
            in_specs=[
                pl.BlockSpec((1, rows_home, 2 * FF), lambda i: (i, 0, 0)),
                pl.BlockSpec((spare, rows_home, 2 * FF), lambda i: (planes // spare, 0, 0)),
                pl.BlockSpec((1, piece, D), lambda i: (i, 0, 0)),
                pl.BlockSpec((spare, piece, D), lambda i: (planes // spare, 0, 0)),
            ],
            out_specs=[
                pl.BlockSpec((planes, rows_home, packed_columns), lambda i: (0, 0, 0)),
                pl.BlockSpec((narrow, D), lambda i: (0, 0)),
            ],
            out_shape=[
                jax.ShapeDtypeStruct((planes, rows_home, packed_columns), bf16),
                jax.ShapeDtypeStruct((narrow, D), bf16),
            ],
            cost_estimate=pl.CostEstimate(flops=0, bytes_accessed=2**24, transcendentals=0),
            compiler_params=pltpu.CompilerParams(vmem_limit_bytes=48 * 2**20),
        )(gate_up, gate_up, down, down)

    def down_of(packed, low):
        if not whole:
            return low
        mine = packed[:, 2 * units :].reshape(planes, across, piece, wide)
        mine = mine.transpose(0, 2, 1, 3).reshape(wide, D)
        return jnp.concatenate([mine, low], axis=0)

    def combine_kernel(a_ref, came_a_ref, b_ref, came_b_ref, c_ref, came_c_ref, full_ref, rest_ref, low_ref):
        total = a_ref[...].astype(f32) + came_a_ref[...].astype(f32)
        full_ref[0] = total[:, : 2 * wide].astype(bf16)
        rest_ref[0, :, pl.ds(0, 2 * narrow_pad)] = total[:, 2 * wide :].astype(bf16)
        total = residual_scale * (b_ref[...].astype(f32) + came_b_ref[...].astype(f32))
        for j in range(across):
            rest_ref[0, pl.ds(j * piece, piece), pl.ds(2 * narrow_pad, wide)] = total[
                :, j * wide : (j + 1) * wide
            ].astype(bf16)
        low_ref[...] = residual_scale * (c_ref[...].astype(f32) + came_c_ref[...].astype(f32))

    def combine_grads(gate_up, came_gate_up, down, came_down):
        if not whole:
            total = (gate_up.astype(f32) + came_gate_up.astype(f32)).astype(bf16)
            low = residual_scale * (down.astype(f32) + came_down.astype(f32))
            return None, total.reshape(planes, rows_home, rest), low
        return pl.pallas_call(
            combine_kernel,
            grid=(planes,),
            in_specs=[pl.BlockSpec((rows_home, 2 * units), lambda i: (i, 0))] * 2
            + [pl.BlockSpec((piece, D), lambda i: (i, 0))] * 2
            + [pl.BlockSpec((narrow, D), lambda i: (wide // narrow, 0))] * 2,
            out_specs=[
                pl.BlockSpec((1, rows_home, 2 * FF), lambda i: (i, 0, 0)),
                pl.BlockSpec((1, rows_home, rest), lambda i: (i, 0, 0)),
                pl.BlockSpec((narrow, D), lambda i: (0, 0)),
            ],
            out_shape=[
                jax.ShapeDtypeStruct((planes, rows_home, 2 * FF), bf16),
                jax.ShapeDtypeStruct((planes, rows_home, rest), bf16),
                jax.ShapeDtypeStruct((narrow, D), f32),
            ],
            cost_estimate=pl.CostEstimate(flops=0, bytes_accessed=2**24, transcendentals=0),
            compiler_params=pltpu.CompilerParams(vmem_limit_bytes=48 * 2**20),
        )(gate_up, came_gate_up, down, came_down, down, came_down)

    gate_up_rate = D ** (-0.5)
    down_rate = max(2, FF // 128) ** (-0.5)

    def full_kernel(home_ref, w_ref, m_ref, s_ref, *outs):
        done = adam_step(
            w_ref[0], m_ref[0], s_ref[0], home_ref[0].astype(f32), gate_up_rate, weight_decay
        )
        for ref, value in zip(outs, done):
            ref[0] = value

    def spare_kernel(home_ref, w_ref, m_ref, s_ref, a_ref, b_ref, c_ref, *outs):
        for s in range(spare):

            @pl.when(pl.program_id(0) == s)
            def _():
                grad = jnp.concatenate(
                    [
                        lanes(home_ref[p], g * narrow_pad + s * piece)
                        for g in range(2)
                        for p in range(planes)
                    ],
                    axis=1,
                ).astype(f32)
                done = adam_step(w_ref[0], m_ref[0], s_ref[0], grad, gate_up_rate, weight_decay)
                for ref, value in zip(outs, done):
                    ref[0] = value

    def down_kernel(home_ref, low_ref, w_ref, m_ref, s_ref, *outs):
        def update(grad):
            done = adam_step(w_ref[0], m_ref[0], s_ref[0], grad, down_rate, weight_decay)
            for ref, value in zip(outs, done):
                ref[0] = value

        @pl.when(pl.program_id(0) < planes)
        def _():
            update(
                jnp.concatenate(
                    [
                        home_ref[0, pl.ds(j * piece, piece), pl.ds(2 * narrow_pad, wide)]
                        for j in range(across)
                    ],
                    axis=1,
                ).astype(f32)
            )

        @pl.when(pl.program_id(0) >= planes)
        def _():
            update(low_ref[...])

    def update_experts(home_full, home_rest, low, gate_up, down):
        if not whole:
            grad = join_spare(home_rest).astype(f32)
            return (
                adam_step(*gate_up, grad, gate_up_rate, weight_decay),
                adam_step(
                    *down, low[:narrow].reshape(spare, piece, D), down_rate, weight_decay
                ),
            )
        params = pltpu.CompilerParams(vmem_limit_bytes=48 * 2**20)
        shapes = [jax.ShapeDtypeStruct(gate_up[0].shape, f32)] * 3
        one = pl.BlockSpec((1, rows_home, 2 * FF), lambda i: (i, 0, 0))
        last = pl.BlockSpec((1, rows_home, 2 * FF), lambda i: (planes + i, 0, 0))
        new_gate_up = pl.pallas_call(
            full_kernel,
            grid=(planes,),
            in_specs=[one] * 4,
            out_specs=[one] * 3,
            cost_estimate=pl.CostEstimate(flops=0, bytes_accessed=2**25, transcendentals=0),
            out_shape=shapes,
            compiler_params=params,
        )(home_full, *gate_up)
        new_gate_up = pl.pallas_call(
            spare_kernel,
            grid=(spare,),
            in_specs=[pl.BlockSpec((planes, rows_home, 2 * narrow_pad), lambda i: (0, 0, 0))]
            + [last] * 3
            + [pl.BlockSpec(memory_space=pl.ANY)] * 3,
            out_specs=[last] * 3,
            out_shape=shapes,
            input_output_aliases={4: 0, 5: 1, 6: 2},
            compiler_params=params,
        )(home_rest, *gate_up, *new_gate_up)
        row = pl.BlockSpec((1, piece, D), lambda i: (i, 0, 0))
        new_down = pl.pallas_call(
            down_kernel,
            grid=(per_group,),
            in_specs=[
                pl.BlockSpec((1, rows_home, rest), lambda i: (jnp.minimum(i, planes - 1), 0, 0)),
                pl.BlockSpec((piece, D), lambda i: (jnp.maximum(i - planes, 0), 0)),
            ]
            + [row] * 3,
            out_specs=[row] * 3,
            cost_estimate=pl.CostEstimate(flops=0, bytes_accessed=2**24, transcendentals=0),
            out_shape=[jax.ShapeDtypeStruct(down[0].shape, f32)] * 3,
            compiler_params=params,
        )(home_rest, low, *down)
        return new_gate_up, new_down

    def unit_experts(group, place):
        base = group * per_group
        sets = []
        if whole:
            sets.append(jnp.full((wide,), base + place))
        behind = base + whole * planes + jnp.arange(narrow_pad) // piece
        sets.append(jnp.where(jnp.arange(narrow_pad) < narrow, behind, -1))
        return jnp.concatenate(sets)

    def columns_of():
        pieces = []
        for first in range(0, wide, 256):
            pieces.append((first, wide + first, first, min(256, wide - first)))
        pieces.append((2 * wide, 2 * wide + narrow_pad, wide, narrow_pad))
        return pieces

    def expert_kernel(first_call, *refs):
        rows_ref, gates_ref = refs[:2]
        reaches, weights = refs[2:4], refs[4:6]
        twice_ref, once_ref = refs[6:8]
        gated_ref, grad_ref, two_ref = refs[8 + (0 if first_call else 2) :]
        blocks, rows_of, _ = rows_ref.shape
        count = blocks * rows_of
        rows = rows_ref[...].reshape(count, D)
        gates = gates_ref[...].reshape(count, LANES)
        dgate = jnp.zeros((count, LANES), f32)
        for k in range(2):
            for gate_at, up_at, unit_at, width in columns_of():
                unit = pl.ds(k * units + unit_at, width)
                gate_w = weights[k][:, pl.ds(gate_at, width)]
                up_w = weights[k][:, pl.ds(up_at, width)]
                gate_part = jnp.dot(rows, gate_w, preferred_element_type=f32)
                up_part = jnp.dot(rows, up_w, preferred_element_type=f32)
                gate_wide = jnp.dot(gates, twice_ref[:, unit], preferred_element_type=f32)
                reach = reaches[k][:, :, pl.ds(unit_at, width)].reshape(count, width)
                reach = residual_scale * reach
                squash = 1.0 / (1.0 + jnp.exp(-gate_part))
                swish = gate_part * squash
                hidden = swish * up_part
                gated = (hidden * gate_wide).astype(bf16)
                gated_ref[:, :, unit] = gated.reshape(blocks, rows_of, width)
                dgate += dot_nt((hidden * reach).astype(bf16), once_ref[:, unit])
                grad_hidden = reach * gate_wide
                grad_gate = grad_hidden * up_part * squash * (1.0 + gate_part * (1.0 - squash))
                for at, value in ((gate_at, grad_gate), (up_at, grad_hidden * swish)):
                    grad_ref[:, :, pl.ds(k * 2 * units + at, width)] = value.astype(bf16).reshape(
                        blocks, rows_of, width
                    )
        two = jnp.zeros((count, D), f32)
        for k in range(2):
            grad = grad_ref[:, :, pl.ds(k * 2 * units, 2 * units)].reshape(count, 2 * units)
            two += dot_nt(grad, weights[k][...])
        two_ref[:, :, pl.ds(0, D)] = two.astype(bf16).reshape(blocks, rows_of, D)
        two_ref[:, :, pl.ds(D, LANES)] = dgate.astype(bf16).reshape(blocks, rows_of, LANES)

    def run_experts(at, sent, reach, own, other, twice, once, before):
        blocks, rows_of, _ = sent.shape
        rows_of = rows_of // 2
        tile = max(1, 512 // rows_of)

        def by_rows(columns, column=0):
            return pl.BlockSpec((tile, rows_of, columns), lambda i: (i, at, column))

        def fixed(rows, columns):
            return pl.BlockSpec((rows, columns), lambda i: (0, 0), pipeline_mode=pl.Buffered(1))

        kept = list(before) if before else []
        count = blocks * rows_of
        return pl.pallas_call(
            functools.partial(expert_kernel, not kept),
            grid=(blocks // tile,),
            in_specs=[by_rows(D), by_rows(LANES, D // LANES)]
            + [by_rows(units)] * 2
            + [fixed(D, 2 * units)] * 2
            + [fixed(LANES, 2 * units)] * 2
            + [pl.BlockSpec(memory_space=pl.ANY)] * len(kept),
            out_specs=[
                by_rows(2 * units),
                by_rows(4 * units),
                pl.BlockSpec((tile, rows_of, D + LANES), lambda i: (i, 0, 0)),
            ],
            out_shape=[
                jax.ShapeDtypeStruct((blocks, 2 * rows_of, 2 * units), bf16),
                jax.ShapeDtypeStruct((blocks, 2 * rows_of, 4 * units), bf16),
                jax.ShapeDtypeStruct((blocks, rows_of, D + LANES), bf16),
            ],
            input_output_aliases={8 + i: i for i in range(len(kept))},
            cost_estimate=pl.CostEstimate(
                flops=16 * count * D * units, bytes_accessed=2**25, transcendentals=2 * count * units
            ),
            compiler_params=pltpu.CompilerParams(vmem_limit_bytes=60 * 2**20),
        )(sent, sent, *reach, own, other, twice, once, *kept)

    def shards(
        tokens,
        cotangent,
        routes,
        weight_qkv,
        moment_qkv,
        square_qkv,
        weight_out,
        moment_out,
        square_out,
        weight_router,
        moment_router,
        square_router,
        gains,
        moment_gains,
        square_gains,
        weight_gate_up,
        moment_gate_up,
        square_gate_up,
        weight_down,
        moment_down,
        square_down,
    ):
        sequence_length = tokens.shape[0]
        head_groups = QUERY_HEADS // KEY_VALUE_HEADS
        place = lax.axis_index(PLANE)
        group = lax.axis_index("y") * 2 + lax.axis_index("core")
        partner = lax.axis_index("y") * 2 + 1 - lax.axis_index("core")

        small = pad_lanes(jnp.concatenate([weight_router, gains.T], axis=1))
        first_pack = jnp.concatenate([weight_qkv, small], axis=1).astype(bf16)
        first_all = lax.all_gather(first_pack, ALL, axis=0, tiled=True)

        packed, low_own = pack_experts(weight_gate_up, weight_down)
        out_line = line_of(chip_half(weight_out.astype(bf16)))
        cot_line = line_of(after(cotangent, low_own, out_line[1]))
        own = all_to_all_plane(after(packed, cot_line[-1], out_line[-1])).reshape(D, -1)
        out_mine, out_other = gather_halves(out_line)
        core = lax.axis_index("core")
        order_mine, order_other = row_order(core), row_order(1 - core)
        blocks_order = block_order()

        qkv_w = first_all[:, :QKV]
        router_w = first_all[:, QKV : QKV + EXPERTS]
        gain_one = first_all[:, QKV + EXPERTS].astype(f32)
        gain_two = first_all[:, QKV + EXPERTS + 1].astype(f32)

        inputs = tokens.astype(f32)
        factor_one = lax.rsqrt(jnp.mean(inputs * inputs, axis=-1, keepdims=True) + norm_eps)
        hidden_one = (inputs * factor_one * gain_one).astype(bf16)
        joined_heads = dot(hidden_one, qkv_w)
        cot_all = gather_tokens(cot_line, joined_heads)
        hidden_mine = dot(hidden_one, order_mine).astype(bf16)
        hidden_other = dot(hidden_one, order_other).astype(bf16)
        query_rows = joined_heads[:, :HEADS_WIDTH].reshape(sequence_length, QUERY_HEADS, HEAD_SIZE)
        every_key = joined_heads[:, HEADS_WIDTH : HEADS_WIDTH + KEYS_WIDTH].reshape(
            sequence_length, KEY_VALUE_HEADS, HEAD_SIZE
        )
        every_value = joined_heads[:, HEADS_WIDTH + KEYS_WIDTH :].reshape(
            sequence_length, KEY_VALUE_HEADS, HEAD_SIZE
        )
        cosine_lookup, sine_lookup = rotary_tables(sequence_length, HEAD_SIZE)
        query_rotated = (
            apply_rotation(query_rows, cosine_lookup, sine_lookup)
            .astype(bf16)
            .reshape(sequence_length, KEY_VALUE_HEADS, head_groups, HEAD_SIZE)
        )
        key_rot = apply_rotation(every_key, cosine_lookup, sine_lookup).astype(bf16)
        value_low = every_value.astype(bf16)
        causal = jnp.arange(sequence_length)[:, None] >= jnp.arange(sequence_length)[None, :]
        scores = attention_scores(query_rotated, key_rot, causal)
        peak = jnp.max(scores, axis=-1, keepdims=True)
        expo = jnp.exp(scores - peak)
        totals = jnp.sum(expo, axis=-1, keepdims=True)
        probs = expo / totals
        prob_low = probs.astype(bf16)
        heads = jnp.einsum("kgst,tkd->skgd", prob_low, value_low, preferred_element_type=f32)
        attended = heads.reshape(sequence_length, HEADS_WIDTH).astype(bf16)
        attended_mine = dot(attended, order_mine).astype(bf16)
        attended_other = dot(attended, order_other).astype(bf16)
        projected = [dot(attended_mine, out_mine), dot(attended_other, out_other)]
        mid = inputs + residual_scale * jnp.where(
            core == 0,
            jnp.concatenate(projected, axis=1),
            jnp.concatenate(projected[::-1], axis=1),
        )
        factor_two = lax.rsqrt(jnp.mean(mid * mid, axis=-1, keepdims=True) + norm_eps)
        hidden_two = (mid * factor_two * gain_two).astype(bf16)
        logits = dot(hidden_two, router_w)
        named = jnp.any(
            routes[..., None] == jnp.arange(EXPERTS, dtype=routes.dtype)[None, None, :], axis=1
        )
        shown = jnp.where(named, logits, -jnp.inf)
        raised = jnp.exp(shown - jnp.max(shown, axis=-1, keepdims=True))
        gates = raised / jnp.sum(raised, axis=-1, keepdims=True)

        gate_high = gates.astype(bf16)
        gate_rest = (gates - gate_high.astype(f32)).astype(bf16)
        sent = jnp.concatenate(
            [hidden_two, pad_lanes(jnp.concatenate([gate_high, gate_rest], axis=1))], axis=1
        )
        sent_all = lax.all_gather(sent, SAME_CORE, axis=0, tiled=True)
        sent_all = permute_blocks(sent_all, blocks_order)
        own = after(own, cot_all)
        other, low_other = swap_core(own), swap_core(low_own)
        down_own, down_other = down_of(own, low_own), down_of(other, low_other)
        blocks = 2 * nx * ny
        reach = [dot_nt(cot_all, d).reshape(blocks, -1, units) for d in (down_own, down_other)]

        behind = jnp.concatenate([unit_experts(group, place), unit_experts(partner, place)])
        numbers = jnp.arange(LANES)[:, None]
        real = behind[None, :] >= 0
        once = ((numbers == behind[None, :]) & real).astype(bf16)
        twice = once + ((numbers == behind[None, :] + EXPERTS) & real).astype(bf16)
        kept = None
        firsts = []
        sent_blocks = sent_all.reshape(blocks, -1, sent_all.shape[1])
        for at in range(2):
            *kept, two = run_experts(at, sent_blocks, reach, own, other, twice, once, kept)
            firsts.append(scatter_first(two))
        two_sum = sum_line(scatter_second(firsts))

        gated, grad_both = (k.reshape(-1, k.shape[2]) for k in kept)
        gated, grad_both = after(gated, *firsts[-1], always=True), after(grad_both, *firsts[-1])
        rows_all = after(sent_all, *firsts[-1], always=True)[:, :D]
        mixed = (dot(gated[:, :units], down_own) + dot(gated[:, units:], down_other)).astype(bf16)
        mixed = after(mixed, two_sum, always=True).reshape(blocks, -1, D)
        mixed_first = scatter_first(mixed)

        came_gate_up = swap_core(dot_tn(rows_all, grad_both[:, 2 * units :]).astype(bf16))
        came_down = swap_core(dot_tn(gated[:, units:], cot_all).astype(bf16))
        full, more, low = combine_grads(
            dot_tn(rows_all, grad_both[:, : 2 * units]).astype(bf16),
            came_gate_up,
            dot_tn(gated[:, :units], cot_all).astype(bf16),
            came_down,
        )
        home_full = all_to_all_plane(after(full, two_sum)) if whole else None
        home_rest = all_to_all_plane(after(more, two_sum))
        two_sum = after(two_sum, low)
        grad_two, grad_gates = two_sum[:, :D], two_sum[:, D : D + EXPERTS]

        grad_out = cotangent.astype(f32)
        grad_chosen = gates * (grad_gates - jnp.sum(gates * grad_gates, axis=-1, keepdims=True))
        grad_logits = grad_chosen.astype(bf16)
        grad_router = dot_tn(hidden_two, grad_logits)
        grad_two = grad_two + dot_nt(grad_logits, router_w)
        grad_mid, grad_gain_two = norm_backward(grad_two, mid, factor_two, gain_two)
        grad_mid = grad_out + grad_mid
        grad_att = (residual_scale * grad_mid).astype(bf16)
        att_left, att_right = grad_att[:, : D // 2], grad_att[:, D // 2 :]
        att_mine = jnp.where(core == 0, att_left, att_right)
        att_other = jnp.where(core == 0, att_right, att_left)
        grad_heads = (
            dot_nt(dot_nt(att_mine, out_mine).astype(bf16), order_mine)
            + dot_nt(dot_nt(att_other, out_other).astype(bf16), order_other)
        )
        grad_heads = grad_heads.astype(bf16).reshape(
            sequence_length, KEY_VALUE_HEADS, head_groups, HEAD_SIZE
        )
        out_first = scatter_halves_first(
            dot_tn(attended_mine, att_mine).astype(bf16),
            dot_tn(attended_other, att_other).astype(bf16),
        )
        out_left, out_right = scatter_halves_second(out_first)
        grad_probs = jnp.einsum(
            "skgd,tkd->kgst", grad_heads, value_low, preferred_element_type=f32
        )
        value_gradient = jnp.einsum(
            "kgst,skgd->tkd", prob_low, grad_heads, preferred_element_type=f32
        )
        row_dot = jnp.sum(probs * grad_probs, axis=-1, keepdims=True)
        grad_scores = (probs * (grad_probs - row_dot)).astype(bf16)
        grad_qrot = (
            jnp.einsum("kgst,tkd->skgd", grad_scores, key_rot, preferred_element_type=f32)
            * score_scale
        )
        grad_krot = (
            jnp.einsum("kgst,skgd->tkd", grad_scores, query_rotated, preferred_element_type=f32)
            * score_scale
        )
        grad_queries = apply_rotation(
            grad_qrot.reshape(sequence_length, QUERY_HEADS, HEAD_SIZE), cosine_lookup, -sine_lookup
        )
        key_gradient = apply_rotation(grad_krot, cosine_lookup, -sine_lookup)
        grad_joined = jnp.concatenate(
            [
                grad_queries.reshape(sequence_length, HEADS_WIDTH),
                key_gradient.reshape(sequence_length, KEYS_WIDTH),
                value_gradient.reshape(sequence_length, KEYS_WIDTH),
            ],
            axis=1,
        ).astype(bf16)
        grad_one = dot_nt(grad_joined, qkv_w)
        grad_inputs, grad_gain_one = norm_backward(grad_one, inputs, factor_one, gain_one)
        token_grad = grad_mid + grad_inputs
        small_sent = pad_lanes(
            jnp.concatenate([grad_router, grad_gain_one[:, None], grad_gain_two[:, None]], axis=1)
        )
        small_sent = small_sent.astype(bf16)
        joined_left, joined_right = grad_joined[:, : QKV // 2], grad_joined[:, QKV // 2 :]
        qkv_sent = []
        for hidden, rows_order, at in (
            (hidden_mine, order_mine, core),
            (hidden_other, order_other, 1 - core),
        ):
            product = dot_tn(hidden, jnp.where(at == 0, joined_left, joined_right))
            extra = jnp.where(at == 0, dot_tn(rows_order, small_sent), 0.0)
            qkv_sent.append(jnp.concatenate([product, extra], axis=1).astype(bf16))
        qkv_first = scatter_halves_first(qkv_sent[0], after(qkv_sent[1], out_first, home_full))
        mixed = sum_line(scatter_second([[after(m, qkv_first) for m in mixed_first]]))
        layer_out = (mid + residual_scale * mixed).astype(bf16)
        qkv_left, qkv_right = scatter_halves_second(qkv_first, home_rest)
        sum_out = jnp.concatenate([out_left, out_right], axis=1)
        sum_qkv = jnp.concatenate([qkv_left[:, : QKV // 2], qkv_right[:, : QKV // 2]], axis=1)
        sum_router = qkv_left[:, QKV // 2 : QKV // 2 + EXPERTS]
        sum_gains = qkv_left[:, QKV // 2 + EXPERTS : QKV // 2 + EXPERTS + 2].T

        new_gate_up, new_down = update_experts(
            home_full,
            home_rest,
            low,
            (weight_gate_up, moment_gate_up, square_gate_up),
            (weight_down, moment_down, square_down),
        )
        new_qkv = adam_step(weight_qkv, moment_qkv, square_qkv, sum_qkv, D ** (-0.5), weight_decay)
        new_out = adam_step(
            weight_out,
            moment_out,
            square_out,
            sum_out,
            max(4, QUERY_HEADS * HEAD_SIZE // 256) ** (-0.5),
            weight_decay,
        )
        new_router = adam_step(
            weight_router, moment_router, square_router, sum_router, (4 * D) ** (-0.5), weight_decay
        )
        new_gains = adam_step(gains, moment_gains, square_gains, sum_gains, 0.75, 0.0)
        return (
            layer_out,
            token_grad,
            *new_qkv,
            *new_out,
            *new_router,
            *new_gains,
            *new_gate_up,
            *new_down,
        )

    return shards


def solution(mesh):
    n_dp, n_expert = mesh.shape["dp"], mesh.shape["expert"]
    nz = 4
    nx, ny = n_dp // nz, n_expert // 2
    fine = Mesh(mesh.devices.reshape(nz, nx, ny, 2), ALL)
    rows = P(ALL, None)
    columns = P(None, ALL)
    experts = P(("y", "core"), ("z", "x"), None)
    dense = (rows,) * 9 + (columns,) * 3 + (experts,) * 6
    return jax.shard_map(
        make_shards((nz, nx, ny)),
        mesh=fine,
        in_specs=(rows,) * 3 + dense,
        out_specs=(rows,) * 2 + dense,
        check_vma=False,
    )
```

profile of v0, /device:TPU:0, one launch (start us, length us, event | category | flops | bytes accessed | tf_op | source)
XLA Modules:
  0.0 772.9 jit_solution(5940643483092343826)
XLA Ops:
  15.3 8.5 %shard_map.438 = (bf16[8,192,1792]{2,1,0:T(8,128)(2,1)}, bf16[128,1536]{1,0:T(8,128)(2,1)S(1)}) custom-call(f32[10,192,1024]{2,1,0:T(8,128)} %w_ref.4, f32[10,192,1024]{2,1,0:T(8,128)} %w_ref.4, f32[10,64,1536]{2,1,0:T(8,128)S(1)} %copy-done.2, f32[10,64,1536]{2,1,0:T(8,128)S(1)} %copy-done.2), custom_call_target="tpu_custom_call" | custom-call | bytes 16777216 | tf_op jit(solution)/shard_map/pallas_call | solution.py:373
  28.0 8.3 %collective-permute-done.1.refs_2_ = bf16[96,768]{1,0:T(8,128)(2,1)S(1)} collective-permute-done((bf16[96,768]{1,0:T(8,128)(2,1)S(1)}, bf16[96,768]{1,0:T(8,128)(2,1)S(1)}, u32[]{:S(2)}, u32[]{:S(2)}) %collective-permute-start.1) | collective-permute-done | bytes 147488 | tf_op jit(solution)/shard_map/ppermute | solution.py:151
  36.4 6.5 collective-permute-done.2
  43.0 13.0 %collective-permute-done.3.refs_2_ = bf16[96,768]{1,0:T(8,128)(2,1)S(1)} collective-permute-done((bf16[96,768]{1,0:T(8,128)(2,1)S(1)}, bf16[96,768]{1,0:T(8,128)(2,1)S(1)}, u32[]{:S(2)}, u32[]{:S(2)}) %collective-permute-start.3) | collective-permute-done | bytes 147488 | tf_op jit(solution)/shard_map/ppermute | solution.py:151
  68.5 22.9 %collective-permute-done.8 = bf16[128,1536]{1,0:T(8,128)(2,1)S(1)} collective-permute-done((bf16[128,1536]{1,0:T(8,128)(2,1)S(1)}, bf16[128,1536]{1,0:T(8,128)(2,1)S(1)}, u32[]{:S(2)}, u32[]{:S(2)}) %collective-permute-start.8) | collective-permute-done | bytes 393248 | tf_op jit(solution)/shard_map/ppermute | solution.py:151
  92.5 14.5 %collective-permute-done.9.refs_1_ = bf16[128,1536]{1,0:T(8,128)(2,1)S(1)} collective-permute-done((bf16[128,1536]{1,0:T(8,128)(2,1)S(1)}, bf16[128,1536]{1,0:T(8,128)(2,1)S(1)}, u32[]{:S(2)}, u32[]{:S(2)}) %collective-permute-start.9) | collective-permute-done | bytes 393248 | tf_op jit(solution)/shard_map/ppermute | solution.py:151
  145.1 32.7 %collective-permute-done.10 = bf16[256,1536]{1,0:T(8,128)(2,1)S(1)} collective-permute-done((bf16[256,1536]{1,0:T(8,128)(2,1)}, bf16[256,1536]{1,0:T(8,128)(2,1)S(1)}, u32[]{:S(2)}, u32[]{:S(2)}) %collective-permute-start.10) | collective-permute-done | bytes 786464 | tf_op jit(solution)/shard_map/ppermute | solution.py:151
  184.7 28.8 %collective-permute-done.11 = bf16[512,1536]{1,0:T(8,128)(2,1)S(1)} collective-permute-done((bf16[512,1536]{1,0:T(8,128)(2,1)S(1)}, bf16[512,1536]{1,0:T(8,128)(2,1)S(1)}, u32[]{:S(2)}, u32[]{:S(2)}) %collective-permute-start.11) | collective-permute-done | bytes 1572896 | tf_op jit(solution)/shard_map/ppermute | solution.py:151
  216.6 27.2 %collective-permute-done.13 = bf16[512,1536]{1,0:T(8,128)(2,1)S(1)} collective-permute-done((bf16[512,1536]{1,0:T(8,128)(2,1)S(1)}, bf16[512,1536]{1,0:T(8,128)(2,1)S(1)}, u32[]{:S(2)}, u32[]{:S(2)}) %collective-permute-start.13) | collective-permute-done | bytes 1572896 | tf_op jit(solution)/shard_map/ppermute | solution.py:151
  245.0 15.8 %all-to-all-done = bf16[8,192,1792]{2,1,0:T(8,128)(2,1)} async-done(((bf16[8,192,1792]{2,1,0:T(8,128)(2,1)}), bf16[8,192,1792]{2,1,0:T(8,128)(2,1)}, u32[]{:S(2)}, u32[]{:S(2)}) %all-to-all-start) | async-done | bytes 5505056 | tf_op jit(solution)/shard_map/all_to_all | solution.py:326
  268.0 9.4 %fusion.165 = f32[2048,640]{1,0:T(8,128)} fusion(bf16[2048,1536]{1,0:T(8,128)(2,1)} %constant_dynamic-update-slice_fusion.11.refs_1_, bf16[640,1536]{1,0:T(8,128)(2,1)S(1)} %constant_dynamic-update-slice_fusion.17), kind=kOutput, calls=%fused_computation.360 | convolution fusion | flops 4026531840 | bytes 13500416 | tf_op jit(solution)/shard_map/dot_general | solution.py:91
  282.2 8.7 %fusion.166 = f32[2048,640]{1,0:T(8,128)} fusion(bf16[2048,1536]{1,0:T(8,128)(2,1)} %constant_dynamic-update-slice_fusion.11.refs_1_, bf16[640,1536]{1,0:T(8,128)(2,1)S(1)} %constant_dynamic-update-slice_fusion.19), kind=kOutput, calls=%fused_computation.361 | convolution fusion | flops 4026531840 | bytes 13500416 | tf_op jit(solution)/shard_map/dot_general | solution.py:91
  291.0 19.9 %all-gather.5.cloned.1.call-done = bf16[2048,1664]{1,0:T(8,128)(2,1)} async-done(((bf16[128,1664]{1,0:T(8,128)(2,1)}), bf16[2048,1664]{1,0:T(8,128)(2,1)}) %all-gather.5.cloned.1.call-update) | async-done | bytes 6815760 | tf_op jit(solution)/shard_map/all_gather | solution.py:729
  317.8 28.3 %shard_map.444 = (bf16[8,256,1280]{2,1,0:T(8,128)(2,1)}, bf16[8,256,2560]{2,1,0:T(8,128)(2,1)}, bf16[8,128,1664]{2,1,0:T(8,128)(2,1)}) custom-call(bf16[8,256,1664]{2,1,0:T(8,128)(2,1)} %bitcast.180, bf16[8,256,1664]{2,1,0:T(8,128)(2,1)} %bitcast.181, f32[8,256,640]{2,1,0:T(8,128)} %bitcast.214, f32[8,256,640]{2,1,0:T(8,128)} %bitcast.216, ...), custom_call_target="tpu_custom_call" | custom-call | flops 16106127360 | bytes 33554432 | tf_op jit(solution)/shard_map/pallas_call | solution.py:603
  346.1 28.5 %shard_map.445 = (bf16[8,256,1280]{2,1,0:T(8,128)(2,1)}, bf16[8,256,2560]{2,1,0:T(8,128)(2,1)}, bf16[8,128,1664]{2,1,0:T(8,128)(2,1)}) custom-call(bf16[8,256,1664]{2,1,0:T(8,128)(2,1)} %bitcast.182, bf16[8,256,1664]{2,1,0:T(8,128)(2,1)} %bitcast.183, f32[8,256,640]{2,1,0:T(8,128)} %bitcast.215, ...), custom_call_target="tpu_custom_call", output_to_operand_aliasing={{0}: (8, {}), {1}: (9, {})} | custom-call | flops 16106127360 | bytes 33554432 | tf_op jit(solution)/shard_map/pallas_call | solution.py:603
  380.6 17.6 %collective-permute-done.16 = bf16[2,128,1664]{2,1,0:T(8,128)(2,1)S(1)} collective-permute-done((bf16[2,128,1664]{2,1,0:T(8,128)(2,1)S(1)}, bf16[2,128,1664]{2,1,0:T(8,128)(2,1)S(1)}, u32[]{:S(2)}, u32[]{:S(2)}) %collective-permute-start.16) | collective-permute-done | bytes 852000 | tf_op jit(solution)/shard_map/ppermute | solution.py:151
  401.4 13.7 %convolution_convert_fusion.2 = bf16[1536,1280]{1,0:T(8,128)(2,1)} fusion(bf16[2048,1664]{1,0:T(8,128)(2,1)} %shard_map.448, bf16[2048,2560]{1,0:T(8,128)(2,1)} %shard_map.449), kind=kOutput, calls=%fused_computation.15 | convolution fusion | flops 8055029760 | bytes 15466496 | tf_op jit(solution)/shard_map/dot_general | solution.py:95
  415.1 10.7 %convolution_convert_fusion.3.a_ref = bf16[1536,1280]{1,0:T(8,128)(2,1)} fusion(bf16[2048,1664]{1,0:T(8,128)(2,1)S(1)} %copy-done.6, bf16[2048,2560]{1,0:T(8,128)(2,1)S(1)} %copy-done.27), kind=kOutput, calls=%fused_computation.16 | convolution fusion | flops 8055029760 | bytes 15466496 | tf_op jit(solution)/shard_map/dot_general | solution.py:95
  428.2 9.2 %convolution_convert_fusion.6 = bf16[640,1536]{1,0:T(8,128)(2,1)} fusion(bf16[2048,1536]{1,0:T(8,128)(2,1)} %constant_dynamic-update-slice_fusion.11.refs_1_, bf16[2048,1280]{1,0:T(8,128)(2,1)} %shard_map.446), kind=kOutput, calls=%fused_computation.41 | convolution fusion | flops 4027514880 | bytes 10878976 | tf_op jit(solution)/shard_map/dot_general | solution.py:95
  458.2 7.0 add_convert_fusion.refs_0_
  469.4 8.3 %convolution_convert_fusion.7.b_ref.c_ref = bf16[640,1536]{1,0:T(8,128)(2,1)} fusion(bf16[2048,1536]{1,0:T(8,128)(2,1)} %constant_dynamic-update-slice_fusion.11.refs_1_, bf16[2048,1280]{1,0:T(8,128)(2,1)S(1)} %copy-done.33), kind=kOutput, calls=%fused_computation.42 | convolution fusion | flops 4027514880 | bytes 10878976 | tf_op jit(solution)/shard_map/dot_general | solution.py:95
  480.2 8.2 %shard_map.450 = (bf16[8,192,1024]{2,1,0:T(8,128)(2,1)}, bf16[8,192,768]{2,1,0:T(8,128)(2,1)}, f32[128,1536]{1,0:T(8,128)S(1)}) custom-call(bf16[1536,1280]{1,0:T(8,128)(2,1)} %convolution_convert_fusion.3.a_ref, bf16[1536,1280]{1,0:T(8,128)(2,1)} %collective-permute-done.26.came_a_ref, bf16[640,1536]{1,0:T(8,128)(2,1)S(1)} %copy-done.7, ...), custom_call_target="tpu_custom_call" | custom-call | bytes 16777216 | tf_op jit(solution)/shard_map/pallas_call | solution.py:417
  521.2 7.5 fusion.78
  536.2 6.3 convolution_convert_fusion.1
  551.6 9.6 %all-to-all-done.1.refs_2_.home_ref = bf16[8,192,1024]{2,1,0:T(8,128)(2,1)S(1)} async-done(((bf16[8,192,1024]{2,1,0:T(8,128)(2,1)}), bf16[8,192,1024]{2,1,0:T(8,128)(2,1)S(1)}, u32[]{:S(2)}, u32[]{:S(2)}) %all-to-all-start.1) | async-done | bytes 3145760 | tf_op jit(solution)/shard_map/all_to_all | solution.py:326
  582.5 6.4 convolution_convert_fusion
  597.5 27.0 %collective-permute-done.44 = bf16[96,768]{1,0:T(8,128)(2,1)S(1)} collective-permute-done((bf16[96,768]{1,0:T(8,128)(2,1)S(1)}, bf16[96,768]{1,0:T(8,128)(2,1)S(1)}, u32[]{:S(2)}, u32[]{:S(2)}) %collective-permute-start.44) | collective-permute-done | bytes 147488 | tf_op jit(solution)/shard_map/ppermute | solution.py:151
  645.7 13.6 %shard_map.461 = (f32[10,64,1536]{2,1,0:T(8,128)}, f32[10,64,1536]{2,1,0:T(8,128)}, f32[10,64,1536]{2,1,0:T(8,128)}) custom-call(bf16[8,192,768]{2,1,0:T(8,128)(2,1)S(1)} %all-to-all-done.2.refs_1_.home_ref, f32[128,1536]{1,0:T(8,128)S(1)} %copy-done.9, f32[10,64,1536]{2,1,0:T(8,128)} %w_ref.5, f32[10,64,1536]{2,1,0:T(8,128)} %m_ref.5, f32[10,64,1536]{2,1,0:T(8,128)} %s_ref.5), custom_call_target="tpu_custom_call" | custom-call | bytes 16777216 | tf_op jit(solution)/shard_map/pallas_call | solution.py:520
  669.3 16.0 %shard_map.459 = (f32[10,192,1024]{2,1,0:T(8,128)}, f32[10,192,1024]{2,1,0:T(8,128)}, f32[10,192,1024]{2,1,0:T(8,128)}) custom-call(bf16[8,192,1024]{2,1,0:T(8,128)(2,1)S(1)} %copy-done.4, f32[10,192,1024]{2,1,0:T(8,128)} %w_ref.4, f32[10,192,1024]{2,1,0:T(8,128)} %m_ref.4, f32[10,192,1024]{2,1,0:T(8,128)} %s_ref.4), custom_call_target="tpu_custom_call" | custom-call | bytes 33554432 | tf_op jit(solution)/shard_map/pallas_call | solution.py:499
  696.3 17.1 %collective-permute-done.34 = bf16[1,256,1536]{2,1,0:T(8,128)(2,1)S(1)} collective-permute-done((bf16[1,256,1536]{2,1,0:T(8,128)(2,1)S(1)}, bf16[1,256,1536]{2,1,0:T(8,128)(2,1)S(1)}, u32[]{:S(2)}, u32[]{:S(2)}) %collective-permute-start.34) | collective-permute-done | bytes 786464 | tf_op jit(solution)/shard_map/ppermute | solution.py:151
  733.0 5.8 collective-permute-done.36
  744.7 13.3 %collective-permute-start.42 = (bf16[48,1408]{1,0:T(8,128)(2,1)S(1)}, bf16[48,1408]{1,0:T(8,128)(2,1)S(1)}, u32[]{:S(2)}, u32[]{:S(2)}) collective-permute-start(bf16[48,1408]{1,0:T(8,128)(2,1)S(1)} %broadcast_select_fusion.2), channel_id=1, source_target_pairs={{0,1},{1,0},{2,3},{3,2},{4,5},{5,4},{6,7},{7,6},{8,9},{9,8},{10,11... | collective-permute-start | bytes 405512 | tf_op jit(solution)/shard_map/ppermute | solution.py:104
  (589 shorter events, 286.3 us)
Async XLA Ops:
  7.2 107.2 %all-gather.3.cloned.1.call-start = ((), (), s32[]{:S(2)}) async-start(), calls=%async_computation.3 | async-start | bytes 8515584 | tf_op jit(solution)/shard_map/all_gather | solution.py:659
  67.1 46.2 %collective-permute-start.5 = (bf16[768,768]{1,0:T(8,128)(2,1)}, bf16[768,768]{1,0:T(8,128)(2,1)S(1)}, u32[]{:S(2)}, u32[]{:S(2)}) collective-permute-start(bf16[768,768]{1,0:T(8,128)(2,1)} %get-tuple-element.205), channel_id=1, source_target_pairs={{0,2},{1,5},{2,0},{3,7},{4,6},{5,1},{6,4},{7,3},{8,10},{9,13},{10,... | collective-permute-start | bytes 3538952 | tf_op jit(solution)/shard_map/ppermute | solution.py:151
  68.2 23.2 %collective-permute-start.8 = (bf16[128,1536]{1,0:T(8,128)(2,1)S(1)}, bf16[128,1536]{1,0:T(8,128)(2,1)S(1)}, u32[]{:S(2)}, u32[]{:S(2)}) collective-permute-start(bf16[128,1536]{1,0:T(8,128)(2,1)S(1)} %collective-permute-done.7), channel_id=1, source_target_pairs={{0,8},{1,9},{2,10},{3,11},{4,12},{5,13},{6,14},{7,15},{8,24},{9,25... | collective-permute-start | bytes 1179656 | tf_op jit(solution)/shard_map/ppermute | solution.py:151
  107.7 153.1 %all-to-all-start = ((bf16[8,192,1792]{2,1,0:T(8,128)(2,1)}), bf16[8,192,1792]{2,1,0:T(8,128)(2,1)}, u32[]{:S(2)}, u32[]{:S(2)}) async-start(bf16[8,192,1792]{2,1,0:T(8,128)(2,1)} %shard_map.442), calls=%async_computation | async-start | bytes 11010048 | tf_op jit(solution)/shard_map/all_to_all | solution.py:326
  113.0 197.8 %all-gather.5.cloned.1.call-start = ((), (), s32[]{:S(2)}) async-start(), calls=%async_computation.4 | async-start | bytes 7241728 | tf_op jit(solution)/shard_map/all_gather | solution.py:729
  114.4 17.9 %collective-permute-start.6 = (bf16[1536,768]{1,0:T(8,128)(2,1)}, bf16[1536,768]{1,0:T(8,128)(2,1)}, u32[]{:S(2)}, u32[]{:S(2)}) collective-permute-start(bf16[1536,768]{1,0:T(8,128)(2,1)} %constant_dynamic-update-slice_fusion.5), channel_id=1, source_target_pairs={{0,1},{1,0},{2,3},{3,2},{4,5},{5,4},{6,7},{7,6},{8,9},{9,8},{10,11... | collective-permute-start | bytes 7077896 | tf_op jit(solution)/shard_map/ppermute | solution.py:104
  140.1 37.7 %collective-permute-start.10 = (bf16[256,1536]{1,0:T(8,128)(2,1)}, bf16[256,1536]{1,0:T(8,128)(2,1)S(1)}, u32[]{:S(2)}, u32[]{:S(2)}) collective-permute-start(bf16[256,1536]{1,0:T(8,128)(2,1)} %shard_map.440), channel_id=1, source_target_pairs={{0,4},{1,5},{2,6},{3,7},{4,0},{5,1},{6,2},{7,3},{8,12},{9,13},{10,... | collective-permute-start | bytes 2359304 | tf_op jit(solution)/shard_map/ppermute | solution.py:151
  143.0 37.4 %collective-permute-start.12 = (bf16[256,1536]{1,0:T(8,128)(2,1)}, bf16[256,1536]{1,0:T(8,128)(2,1)S(1)}, u32[]{:S(2)}, u32[]{:S(2)}) collective-permute-start(bf16[256,1536]{1,0:T(8,128)(2,1)} %shard_map.441), channel_id=1, source_target_pairs={{0,2},{1,3},{2,0},{3,1},{4,6},{5,7},{6,4},{7,5},{8,10},{9,11},{10,... | collective-permute-start | bytes 2359304 | tf_op jit(solution)/shard_map/ppermute | solution.py:151
  177.9 35.6 %collective-permute-start.11 = (bf16[512,1536]{1,0:T(8,128)(2,1)S(1)}, bf16[512,1536]{1,0:T(8,128)(2,1)S(1)}, u32[]{:S(2)}, u32[]{:S(2)}) collective-permute-start(bf16[512,1536]{1,0:T(8,128)(2,1)S(1)} %pad_maximum_fusion.1), channel_id=1, source_target_pairs={{0,2},{1,3},{2,0},{3,1},{4,6},{5,7},{6,4},{7,5},{8,10},{9,11},{10,... | collective-permute-start | bytes 4718600 | tf_op jit(solution)/shard_map/ppermute | solution.py:151
  180.5 63.3 %collective-permute-start.13 = (bf16[512,1536]{1,0:T(8,128)(2,1)S(1)}, bf16[512,1536]{1,0:T(8,128)(2,1)S(1)}, u32[]{:S(2)}, u32[]{:S(2)}) collective-permute-start(bf16[512,1536]{1,0:T(8,128)(2,1)S(1)} %pad_maximum_fusion.2), channel_id=1, source_target_pairs={{0,4},{1,5},{2,6},{3,7},{4,0},{5,1},{6,2},{7,3},{8,12},{9,13},{10,... | collective-permute-start | bytes 4718600 | tf_op jit(solution)/shard_map/ppermute | solution.py:151
  260.8 16.6 %collective-permute-start.14 = (bf16[1536,1792]{1,0:T(8,128)(2,1)}, bf16[1536,1792]{1,0:T(8,128)(2,1)}, u32[]{:S(2)}, u32[]{:S(2)}) collective-permute-start(bf16[1536,1792]{1,0:T(8,128)(2,1)} %shard_map.443.refs_4_), channel_id=1, source_target_pairs={{0,1},{1,0},{2,3},{3,2},{4,5},{5,4},{6,7},{7,6},{8,9},{9,8},{10,11... | collective-permute-start | bytes 16515080 | tf_op jit(solution)/shard_map/ppermute | solution.py:104
  261.8 19.1 %collective-permute-start.15 = (bf16[128,1536]{1,0:T(8,128)(2,1)S(1)}, bf16[128,1536]{1,0:T(8,128)(2,1)S(1)}, u32[]{:S(2)}, u32[]{:S(2)}) collective-permute-start(bf16[128,1536]{1,0:T(8,128)(2,1)S(1)} %copy-done.11), channel_id=1, source_target_pairs={{0,1},{1,0},{2,3},{3,2},{4,5},{5,4},{6,7},{7,6},{8,9},{9,8},{10,11... | collective-permute-start | bytes 1179656 | tf_op jit(solution)/shard_map/ppermute | solution.py:104
  376.3 22.0 %collective-permute-start.16 = (bf16[2,128,1664]{2,1,0:T(8,128)(2,1)S(1)}, bf16[2,128,1664]{2,1,0:T(8,128)(2,1)S(1)}, u32[]{:S(2)}, u32[]{:S(2)}) collective-permute-start(bf16[2,128,1664]{2,1,0:T(8,128)(2,1)S(1)} %get-tuple-element.180), channel_id=1, source_target_pairs={{0,2},{1,3},{2,0},{3,1},{4,6},{5,7},{6,4},{7,5},{8,10},{9,11},{10,... | collective-permute-start | bytes 2555912 | tf_op jit(solution)/shard_map/ppermute | solution.py:151
  377.8 21.9 %collective-permute-start.17 = (bf16[2,128,1664]{2,1,0:T(8,128)(2,1)S(1)}, bf16[2,128,1664]{2,1,0:T(8,128)(2,1)S(1)}, u32[]{:S(2)}, u32[]{:S(2)}) collective-permute-start(bf16[2,128,1664]{2,1,0:T(8,128)(2,1)S(1)} %get-tuple-element.179), channel_id=1, source_target_pairs={{0,4},{1,5},{2,6},{3,7},{4,0},{5,1},{6,2},{7,3},{8,12},{9,13},{10,... | collective-permute-start | bytes 2555912 | tf_op jit(solution)/shard_map/ppermute | solution.py:151
  378.5 47.3 %collective-permute-start.18 = (bf16[2,128,1664]{2,1,0:T(8,128)(2,1)S(1)}, bf16[2,128,1664]{2,1,0:T(8,128)(2,1)S(1)}, u32[]{:S(2)}, u32[]{:S(2)}) collective-permute-start(bf16[2,128,1664]{2,1,0:T(8,128)(2,1)S(1)} %get-tuple-element.175), channel_id=1, source_target_pairs={{0,2},{1,3},{2,0},{3,1},{4,6},{5,7},{6,4},{7,5},{8,10},{9,11},{10,... | collective-permute-start | bytes 2555912 | tf_op jit(solution)/shard_map/ppermute | solution.py:151
  378.9 46.8 %collective-permute-start.20 = (bf16[2,128,1664]{2,1,0:T(8,128)(2,1)S(1)}, bf16[2,128,1664]{2,1,0:T(8,128)(2,1)S(1)}, u32[]{:S(2)}, u32[]{:S(2)}) collective-permute-start(bf16[2,128,1664]{2,1,0:T(8,128)(2,1)S(1)} %get-tuple-element.176), channel_id=1, source_target_pairs={{0,4},{1,5},{2,6},{3,7},{4,0},{5,1},{6,2},{7,3},{8,12},{9,13},{10,... | collective-permute-start | bytes 2555912 | tf_op jit(solution)/shard_map/ppermute | solution.py:151
  427.7 16.4 %collective-permute-start.21 = (bf16[1,256,1664]{2,1,0:T(8,128)(2,1)S(1)}, bf16[1,256,1664]{2,1,0:T(8,128)(2,1)}, u32[]{:S(2)}, u32[]{:S(2)}) collective-permute-start(bf16[1,256,1664]{2,1,0:T(8,128)(2,1)S(1)} %fusion.68), channel_id=1, source_target_pairs={{0,2},{1,3},{2,0},{3,1},{4,6},{5,7},{6,4},{7,5},{8,10},{9,11},{10,... | collective-permute-start | bytes 2555912 | tf_op jit(solution)/shard_map/ppermute | solution.py:151
  428.2 50.5 %collective-permute-start.26 = (bf16[1536,1280]{1,0:T(8,128)(2,1)}, bf16[1536,1280]{1,0:T(8,128)(2,1)}, u32[]{:S(2)}, u32[]{:S(2)}) collective-permute-start(bf16[1536,1280]{1,0:T(8,128)(2,1)} %convolution_convert_fusion.2), channel_id=1, source_target_pairs={{0,1},{1,0},{2,3},{3,2},{4,5},{5,4},{6,7},{7,6},{8,9},{9,8},{10,11... | collective-permute-start | bytes 11796488 | tf_op jit(solution)/shard_map/ppermute | solution.py:104
  454.1 24.6 %collective-permute-start.27 = (bf16[640,1536]{1,0:T(8,128)(2,1)}, bf16[640,1536]{1,0:T(8,128)(2,1)S(1)}, u32[]{:S(2)}, u32[]{:S(2)}) collective-permute-start(bf16[640,1536]{1,0:T(8,128)(2,1)} %convolution_convert_fusion.6), channel_id=1, source_target_pairs={{0,1},{1,0},{2,3},{3,2},{4,5},{5,4},{6,7},{7,6},{8,9},{9,8},{10,11... | collective-permute-start | bytes 5898248 | tf_op jit(solution)/shard_map/ppermute | solution.py:104
  489.3 71.9 %all-to-all-start.1 = ((bf16[8,192,1024]{2,1,0:T(8,128)(2,1)}), bf16[8,192,1024]{2,1,0:T(8,128)(2,1)S(1)}, u32[]{:S(2)}, u32[]{:S(2)}) async-start(bf16[8,192,1024]{2,1,0:T(8,128)(2,1)} %shard_map.452), calls=%async_computation.1 | async-start | bytes 6291456 | tf_op jit(solution)/shard_map/all_to_all | solution.py:326
  532.4 16.5 %collective-permute-start.29 = (bf16[2,384,768]{2,1,0:T(8,128)(2,1)}, bf16[2,384,768]{2,1,0:T(8,128)(2,1)}, u32[]{:S(2)}, u32[]{:S(2)}) collective-permute-start(bf16[2,384,768]{2,1,0:T(8,128)(2,1)} %bitcast.53), channel_id=1, source_target_pairs={{0,2},{1,5},{2,0},{3,7},{4,6},{5,1},{6,4},{7,3},{8,10},{9,13},{10,... | collective-permute-start | bytes 3538952 | tf_op jit(solution)/shard_map/ppermute | solution.py:151
  562.9 65.2 %collective-permute-start.30 = (bf16[1536,1408]{1,0:T(8,128)(2,1)}, bf16[1536,1408]{1,0:T(8,128)(2,1)}, u32[]{:S(2)}, u32[]{:S(2)}) collective-permute-start(bf16[1536,1408]{1,0:T(8,128)(2,1)} %shard_map.453), channel_id=1, source_target_pairs={{0,1},{1,0},{2,3},{3,2},{4,5},{5,4},{6,7},{7,6},{8,9},{9,8},{10,11... | collective-permute-start | bytes 12976136 | tf_op jit(solution)/shard_map/ppermute | solution.py:104
  569.0 20.0 %collective-permute-start.43 = (bf16[384,768]{1,0:T(8,128)(2,1)}, bf16[384,768]{1,0:T(8,128)(2,1)}, u32[]{:S(2)}, u32[]{:S(2)}) collective-permute-start(bf16[384,768]{1,0:T(8,128)(2,1)} %slice_bitcast_fusion.3), channel_id=1, source_target_pairs={{0,4},{1,3},{2,6},{3,1},{4,0},{5,7},{6,2},{7,5},{8,12},{9,11},{10,... | collective-permute-start | bytes 1769480 | tf_op jit(solution)/shard_map/ppermute | solution.py:151
  576.1 59.4 %collective-permute-start.25 = (bf16[2,256,1536]{2,1,0:T(8,128)(2,1)}, bf16[2,256,1536]{2,1,0:T(8,128)(2,1)}, u32[]{:S(2)}, u32[]{:S(2)}) collective-permute-start(bf16[2,256,1536]{2,1,0:T(8,128)(2,1)} %bitcast.32), channel_id=1, source_target_pairs={{0,2},{1,3},{2,0},{3,1},{4,6},{5,7},{6,4},{7,5},{8,10},{9,11},{10,... | collective-permute-start | bytes 4718600 | tf_op jit(solution)/shard_map/ppermute | solution.py:151
  578.4 60.5 %collective-permute-start.33 = (bf16[2,256,1536]{2,1,0:T(8,128)(2,1)}, bf16[2,256,1536]{2,1,0:T(8,128)(2,1)}, u32[]{:S(2)}, u32[]{:S(2)}) collective-permute-start(bf16[2,256,1536]{2,1,0:T(8,128)(2,1)} %bitcast.58), channel_id=1, source_target_pairs={{0,4},{1,5},{2,6},{3,7},{4,0},{5,1},{6,2},{7,3},{8,12},{9,13},{10,... | collective-permute-start | bytes 4718600 | tf_op jit(solution)/shard_map/ppermute | solution.py:151
  578.9 66.8 %all-to-all-start.2 = ((bf16[8,192,768]{2,1,0:T(8,128)(2,1)}), bf16[8,192,768]{2,1,0:T(8,128)(2,1)S(1)}, u32[]{:S(2)}, u32[]{:S(2)}) async-start(bf16[8,192,768]{2,1,0:T(8,128)(2,1)} %shard_map.456), calls=%async_computation.2 | async-start | bytes 4718592 | tf_op jit(solution)/shard_map/all_to_all | solution.py:326
  591.9 32.6 %collective-permute-start.44 = (bf16[96,768]{1,0:T(8,128)(2,1)S(1)}, bf16[96,768]{1,0:T(8,128)(2,1)S(1)}, u32[]{:S(2)}, u32[]{:S(2)}) collective-permute-start(bf16[96,768]{1,0:T(8,128)(2,1)S(1)} %slice.594), channel_id=1, source_target_pairs={{0,16},{1,17},{2,18},{3,19},{4,20},{5,21},{6,22},{7,23},{8,0},{9,1... | collective-permute-start | bytes 442376 | tf_op jit(solution)/shard_map/ppermute | solution.py:151
  633.5 27.1 %collective-permute-start.31 = (bf16[2,384,1408]{2,1,0:T(8,128)(2,1)}, bf16[2,384,1408]{2,1,0:T(8,128)(2,1)}, u32[]{:S(2)}, u32[]{:S(2)}) collective-permute-start(bf16[2,384,1408]{2,1,0:T(8,128)(2,1)} %bitcast.55), channel_id=1, source_target_pairs={{0,2},{1,5},{2,0},{3,7},{4,6},{5,1},{6,4},{7,3},{8,10},{9,13},{10,... | collective-permute-start | bytes 6488072 | tf_op jit(solution)/shard_map/ppermute | solution.py:151
  665.4 29.5 %collective-permute-start.32 = (bf16[1,256,1536]{2,1,0:T(8,128)(2,1)S(1)}, bf16[1,256,1536]{2,1,0:T(8,128)(2,1)}, u32[]{:S(2)}, u32[]{:S(2)}) collective-permute-start(bf16[1,256,1536]{2,1,0:T(8,128)(2,1)S(1)} %slice.567), channel_id=1, source_target_pairs={{0,4},{1,5},{2,6},{3,7},{4,0},{5,1},{6,2},{7,3},{8,12},{9,13},{10,... | collective-permute-start | bytes 2359304 | tf_op jit(solution)/shard_map/ppermute | solution.py:151
  691.2 22.4 %collective-permute-start.38 = (bf16[384,1408]{1,0:T(8,128)(2,1)}, bf16[384,1408]{1,0:T(8,128)(2,1)S(1)}, u32[]{:S(2)}, u32[]{:S(2)}) collective-permute-start(bf16[384,1408]{1,0:T(8,128)(2,1)} %slice_bitcast_fusion.1), channel_id=1, source_target_pairs={{0,4},{1,3},{2,6},{3,1},{4,0},{5,7},{6,2},{7,5},{8,12},{9,11},{10,... | collective-permute-start | bytes 3244040 | tf_op jit(solution)/shard_map/ppermute | solution.py:151
  692.8 20.5 %collective-permute-start.34 = (bf16[1,256,1536]{2,1,0:T(8,128)(2,1)S(1)}, bf16[1,256,1536]{2,1,0:T(8,128)(2,1)S(1)}, u32[]{:S(2)}, u32[]{:S(2)}) collective-permute-start(bf16[1,256,1536]{2,1,0:T(8,128)(2,1)S(1)} %slice.572), channel_id=1, source_target_pairs={{0,2},{1,3},{2,0},{3,1},{4,6},{5,7},{6,4},{7,5},{8,10},{9,11},{10,... | collective-permute-start | bytes 2359304 | tf_op jit(solution)/shard_map/ppermute | solution.py:151
  738.9 19.0 %collective-permute-start.37 = (bf16[128,1536]{1,0:T(8,128)(2,1)S(1)}, bf16[128,1536]{1,0:T(8,128)(2,1)S(1)}, u32[]{:S(2)}, u32[]{:S(2)}) collective-permute-start(bf16[128,1536]{1,0:T(8,128)(2,1)S(1)} %add_convert_fusion.16), channel_id=1, source_target_pairs={{0,16},{1,17},{2,18},{3,19},{4,20},{5,21},{6,22},{7,23},{8,0},{9,1... | collective-permute-start | bytes 1179656 | tf_op jit(solution)/shard_map/ppermute | solution.py:151
  (160 other events, 1581.5 us)
Sparse Core Ops, SparseCore 0:
  11.6 96.6 all-gather.2
  139.1 171.7 all-gather.4
where the time goes:
time: 781 us; the launch traced here: 773 us
  waiting for transfers between devices  297 us (38%)
  matrix products  135 us (17%)
  Pallas kernels  109 us (14%)
  starting transfers between devices  85.5 us (11%)
  local copies, waits for them, and re-layouts  75.6 us (10%)
  other arithmetic  54.5 us (7%)
  between operations  16.5 us (2%)
    ppermute x38, waiting for transfers between devices, move(): return lax.ppermute(values, ALL, pairs_of(axes, step))  251 us
    dot_general x11, matrix products, dot_tn(): lax.dot_general(a, b, (((0,), (0,)), ((), ())), preferred_element_type=f32)  64.8 us
    ppermute x38, starting transfers between devices, move(): return lax.ppermute(values, ALL, pairs_of(axes, step))  58.4 us
    pallas_call x2, Pallas kernels, run_experts(): pl.pallas_call(functools.partial(expert_kernel, not kept), grid=(blocks /...  56.7 us
    unnamed x303, local copies, waits for them, and re-layouts  39.9 us
    dot_general x6, matrix products, dot_nt(): lax.dot_general(a, b, (((1,), (1,)), ((), ())), preferred_element_type=f32)  39.6 us
    all_to_all x3, waiting for transfers between devices, all_to_all_plane(): lax.all_to_all(values, PLANE, split_axis=0, concat_axis=0, tiled=True)  26.4 us
    dot_general x8, matrix products, dot(): return jnp.dot(a, b, preferred_element_type=f32)  26.3 us
  transfers between devices with their start and end apart: 53, of which 28 were waited for; matrix products, arithmetic and copies ran while one was open for 29% of the time, Pallas kernels for 6%

commit v1 on v0

--- a/solution.py
+++ b/solution.py
@@ -292,23 +292,31 @@
             acc = grid[s] if acc is None else add_low(move(acc, "yx", -1), grid[s])
         return acc
 
-    def scatter_halves_second(acc, *late):
-        core = lax.axis_index("core")
-        rows = acc.shape[1] // (nz * 2)
+    def scatter_halves_second(acc):
         two = None
         for s in reversed(range(nx)):
             two = acc[s] if two is None else add_low(move(two, "xy", -1), acc[s])
-        two = after(two, *late)
+        return two
+
+    def scatter_halves_line(twos, *late):
+        core = lax.axis_index("core")
+        two = after(jnp.concatenate(twos, axis=1), *late)
+        rows = two.shape[0] // (nz * 2)
         total = None
         for s in reversed(range(nz)):
             mine = two[s * 2 * rows : (s + 1) * 2 * rows]
             total = mine if total is None else add_low(move(total, "zz", -1), mine)
         kept = jnp.where(core == 0, total[:rows], total[rows:])
         came = swap_core(jnp.where(core == 0, total[rows:], total[:rows]))
-        return (
-            jnp.where(core == 0, kept, came).astype(f32),
-            jnp.where(core == 0, came, kept).astype(f32),
-        )
+        left = jnp.where(core == 0, kept, came).astype(f32)
+        right = jnp.where(core == 0, came, kept).astype(f32)
+        found = []
+        at = 0
+        for part in twos:
+            end = at + part.shape[1]
+            found.append((left[:, at:end], right[:, at:end]))
+            at = end
+        return found
 
     def after(values, *first, always=False):
         if not (whole or always):
@@ -789,7 +797,7 @@
             dot_tn(attended_mine, att_mine).astype(bf16),
             dot_tn(attended_other, att_other).astype(bf16),
         )
-        out_left, out_right = scatter_halves_second(out_first)
+        out_two = scatter_halves_second(out_first)
         grad_probs = jnp.einsum(
             "skgd,tkd->kgst", grad_heads, value_low, preferred_element_type=f32
         )
@@ -834,10 +842,12 @@
             product = dot_tn(hidden, jnp.where(at == 0, joined_left, joined_right))
             extra = jnp.where(at == 0, dot_tn(rows_order, small_sent), 0.0)
             qkv_sent.append(jnp.concatenate([product, extra], axis=1).astype(bf16))
-        qkv_first = scatter_halves_first(qkv_sent[0], after(qkv_sent[1], out_first, home_full))
+        qkv_first = scatter_halves_first(qkv_sent[0], after(qkv_sent[1], out_two, home_full, *mixed_first))
         mixed = sum_line(scatter_second([[after(m, qkv_first) for m in mixed_first]]))
         layer_out = (mid + residual_scale * mixed).astype(bf16)
-        qkv_left, qkv_right = scatter_halves_second(qkv_first, home_rest)
+        (out_left, out_right), (qkv_left, qkv_right) = scatter_halves_line(
+            [out_two, scatter_halves_second(qkv_first)], home_rest
+        )
         sum_out = jnp.concatenate([out_left, out_right], axis=1)
         sum_qkv = jnp.concatenate([qkv_left[:, : QKV // 2], qkv_right[:, : QKV // 2]], axis=1)
         sum_router = qkv_left[:, QKV // 2 : QKV // 2 + EXPERTS]

time: 781 us -> 805 us (1.031)
  starting transfers between devices: 85.5 us -> 100 us
  waiting for transfers between devices: 297 us -> 308 us
    ppermute x38 -> x35, waiting for transfers between devices: 251 us -> 269 us  [move(): return lax.ppermute(values, ALL, pairs_of(axes, step))]
    ppermute x10 -> x9, starting transfers between devices: 14 us -> 27.8 us  [swap_core(): return lax.ppermute(values, 'core', [(0, 1), (1, 0)])]
    convert_element_type x23 -> x20, other arithmetic: 25.8 us -> 19.6 us  [add_low(): return (a.astype(f32) + b.astype(f32)).astype(bf16)]
    ppermute x38 -> x35, starting transfers between devices: 58.4 us -> 53.7 us  [move(): return lax.ppermute(values, ALL, pairs_of(axes, step))]
    unnamed x303 -> x307, local copies, waits for them, and re-layouts: 39.9 us -> 44.6 us
  transfers between devices with their start and end apart: 53 -> 49, of which waited for: 28 -> 29; matrix products, arithmetic and copies ran while one was open for 29% -> 27% of each run, Pallas kernels for 6% -> 9%
where the time goes in v1:
time: 805 us; the launch traced here: 795 us
  waiting for transfers between devices  308 us (38%)
  matrix products  132 us (16%)
  Pallas kernels  109 us (14%)
  starting transfers between devices  100 us (12%)
  local copies, waits for them, and re-layouts  77.3 us (10%)
  other arithmetic  51.6 us (6%)
  between operations  16.3 us (2%)
    ppermute x35, waiting for transfers between devices, move(): return lax.ppermute(values, ALL, pairs_of(axes, step))  269 us
    dot_general x11, matrix products, dot_tn(): lax.dot_general(a, b, (((0,), (0,)), ((), ())), preferred_element_type=f32)  62.8 us
    pallas_call x2, Pallas kernels, run_experts(): pl.pallas_call(functools.partial(expert_kernel, not kept), grid=(blocks /...  56.9 us
    ppermute x35, starting transfers between devices, move(): return lax.ppermute(values, ALL, pairs_of(axes, step))  53.7 us
    unnamed x307, local copies, waits for them, and re-layouts  44.6 us
    dot_general x6, matrix products, dot_nt(): lax.dot_general(a, b, (((1,), (1,)), ((), ())), preferred_element_type=f32)  36.3 us
    dot_general x8, matrix products, dot(): return jnp.dot(a, b, preferred_element_type=f32)  28.8 us
    ppermute x9, starting transfers between devices, swap_core(): return lax.ppermute(values, 'core', [(0, 1), (1, 0)])  27.8 us
  transfers between devices with their start and end apart: 49, of which 29 were waited for; matrix products, arithmetic and copies ran while one was open for 27% of the time, Pallas kernels for 9%

profile of v1, /device:TPU:0, one launch (start us, length us, event | category | flops | bytes accessed | tf_op | source)
XLA Modules:
  0.0 795.1 jit_solution(8608875826950020647)
XLA Ops:
  15.3 8.5 %shard_map.438 = (bf16[8,192,1792]{2,1,0:T(8,128)(2,1)}, bf16[128,1536]{1,0:T(8,128)(2,1)S(1)}) custom-call(f32[10,192,1024]{2,1,0:T(8,128)} %w_ref.4, f32[10,192,1024]{2,1,0:T(8,128)} %w_ref.4, f32[10,64,1536]{2,1,0:T(8,128)S(1)} %copy-done.2, f32[10,64,1536]{2,1,0:T(8,128)S(1)} %copy-done.2), custom_call_target="tpu_custom_call" | custom-call | bytes 16777216 | tf_op jit(solution)/shard_map/pallas_call | solution.py:381
  28.0 8.3 %collective-permute-done.1.refs_2_ = bf16[96,768]{1,0:T(8,128)(2,1)S(1)} collective-permute-done((bf16[96,768]{1,0:T(8,128)(2,1)S(1)}, bf16[96,768]{1,0:T(8,128)(2,1)S(1)}, u32[]{:S(2)}, u32[]{:S(2)}) %collective-permute-start.1) | collective-permute-done | bytes 147488 | tf_op jit(solution)/shard_map/ppermute | solution.py:151
  36.4 6.5 collective-permute-done.2
  43.0 13.0 %collective-permute-done.3.refs_2_ = bf16[96,768]{1,0:T(8,128)(2,1)S(1)} collective-permute-done((bf16[96,768]{1,0:T(8,128)(2,1)S(1)}, bf16[96,768]{1,0:T(8,128)(2,1)S(1)}, u32[]{:S(2)}, u32[]{:S(2)}) %collective-permute-start.3) | collective-permute-done | bytes 147488 | tf_op jit(solution)/shard_map/ppermute | solution.py:151
  68.5 22.9 %collective-permute-done.8 = bf16[128,1536]{1,0:T(8,128)(2,1)S(1)} collective-permute-done((bf16[128,1536]{1,0:T(8,128)(2,1)S(1)}, bf16[128,1536]{1,0:T(8,128)(2,1)S(1)}, u32[]{:S(2)}, u32[]{:S(2)}) %collective-permute-start.8) | collective-permute-done | bytes 393248 | tf_op jit(solution)/shard_map/ppermute | solution.py:151
  92.5 14.4 %collective-permute-done.9.refs_1_ = bf16[128,1536]{1,0:T(8,128)(2,1)S(1)} collective-permute-done((bf16[128,1536]{1,0:T(8,128)(2,1)S(1)}, bf16[128,1536]{1,0:T(8,128)(2,1)S(1)}, u32[]{:S(2)}, u32[]{:S(2)}) %collective-permute-start.9) | collective-permute-done | bytes 393248 | tf_op jit(solution)/shard_map/ppermute | solution.py:151
  145.5 32.1 %collective-permute-done.10 = bf16[256,1536]{1,0:T(8,128)(2,1)S(1)} collective-permute-done((bf16[256,1536]{1,0:T(8,128)(2,1)}, bf16[256,1536]{1,0:T(8,128)(2,1)S(1)}, u32[]{:S(2)}, u32[]{:S(2)}) %collective-permute-start.10) | collective-permute-done | bytes 786464 | tf_op jit(solution)/shard_map/ppermute | solution.py:151
  184.7 28.6 %collective-permute-done.11 = bf16[512,1536]{1,0:T(8,128)(2,1)S(1)} collective-permute-done((bf16[512,1536]{1,0:T(8,128)(2,1)S(1)}, bf16[512,1536]{1,0:T(8,128)(2,1)S(1)}, u32[]{:S(2)}, u32[]{:S(2)}) %collective-permute-start.11) | collective-permute-done | bytes 1572896 | tf_op jit(solution)/shard_map/ppermute | solution.py:151
  216.5 26.2 %collective-permute-done.13 = bf16[512,1536]{1,0:T(8,128)(2,1)S(1)} collective-permute-done((bf16[512,1536]{1,0:T(8,128)(2,1)S(1)}, bf16[512,1536]{1,0:T(8,128)(2,1)S(1)}, u32[]{:S(2)}, u32[]{:S(2)}) %collective-permute-start.13) | collective-permute-done | bytes 1572896 | tf_op jit(solution)/shard_map/ppermute | solution.py:151
  243.9 16.6 %all-to-all-done = bf16[8,192,1792]{2,1,0:T(8,128)(2,1)} async-done(((bf16[8,192,1792]{2,1,0:T(8,128)(2,1)}), bf16[8,192,1792]{2,1,0:T(8,128)(2,1)}, u32[]{:S(2)}, u32[]{:S(2)}) %all-to-all-start) | async-done | bytes 5505056 | tf_op jit(solution)/shard_map/all_to_all | solution.py:334
  267.5 9.6 %fusion.162 = f32[2048,640]{1,0:T(8,128)} fusion(bf16[2048,1536]{1,0:T(8,128)(2,1)} %constant_dynamic-update-slice_fusion.11.refs_1_, bf16[640,1536]{1,0:T(8,128)(2,1)S(1)} %constant_dynamic-update-slice_fusion.17), kind=kOutput, calls=%fused_computation.352 | convolution fusion | flops 4026531840 | bytes 13500416 | tf_op jit(solution)/shard_map/dot_general | solution.py:91
  282.0 8.7 %fusion.163 = f32[2048,640]{1,0:T(8,128)} fusion(bf16[2048,1536]{1,0:T(8,128)(2,1)} %constant_dynamic-update-slice_fusion.11.refs_1_, bf16[640,1536]{1,0:T(8,128)(2,1)S(1)} %constant_dynamic-update-slice_fusion.19), kind=kOutput, calls=%fused_computation.353 | convolution fusion | flops 4026531840 | bytes 13500416 | tf_op jit(solution)/shard_map/dot_general | solution.py:91
  290.7 20.2 %all-gather.5.cloned.1.call-done = bf16[2048,1664]{1,0:T(8,128)(2,1)} async-done(((bf16[128,1664]{1,0:T(8,128)(2,1)}), bf16[2048,1664]{1,0:T(8,128)(2,1)}) %all-gather.5.cloned.1.call-update) | async-done | bytes 6815760 | tf_op jit(solution)/shard_map/all_gather | solution.py:737
  317.8 28.2 %shard_map.444 = (bf16[8,256,1280]{2,1,0:T(8,128)(2,1)}, bf16[8,256,2560]{2,1,0:T(8,128)(2,1)}, bf16[8,128,1664]{2,1,0:T(8,128)(2,1)}) custom-call(bf16[8,256,1664]{2,1,0:T(8,128)(2,1)} %bitcast.180, bf16[8,256,1664]{2,1,0:T(8,128)(2,1)} %bitcast.181, f32[8,256,640]{2,1,0:T(8,128)} %bitcast.225, f32[8,256,640]{2,1,0:T(8,128)} %bitcast.227, ...), custom_call_target="tpu_custom_call" | custom-call | flops 16106127360 | bytes 33554432 | tf_op jit(solution)/shard_map/pallas_call | solution.py:611
  350.5 28.7 %shard_map.445 = (bf16[8,256,1280]{2,1,0:T(8,128)(2,1)}, bf16[8,256,2560]{2,1,0:T(8,128)(2,1)}, bf16[8,128,1664]{2,1,0:T(8,128)(2,1)}) custom-call(bf16[8,256,1664]{2,1,0:T(8,128)(2,1)} %bitcast.182, bf16[8,256,1664]{2,1,0:T(8,128)(2,1)} %bitcast.183, f32[8,256,640]{2,1,0:T(8,128)} %bitcast.226, ...), custom_call_target="tpu_custom_call", output_to_operand_aliasing={{0}: (8, {}), {1}: (9, {})} | custom-call | flops 16106127360 | bytes 33554432 | tf_op jit(solution)/shard_map/pallas_call | solution.py:611
  383.5 16.2 %collective-permute-done.16 = bf16[2,128,1664]{2,1,0:T(8,128)(2,1)S(1)} collective-permute-done((bf16[2,128,1664]{2,1,0:T(8,128)(2,1)S(1)}, bf16[2,128,1664]{2,1,0:T(8,128)(2,1)S(1)}, u32[]{:S(2)}, u32[]{:S(2)}) %collective-permute-start.16) | collective-permute-done | bytes 852000 | tf_op jit(solution)/shard_map/ppermute | solution.py:151
  405.7 13.7 %convolution_convert_fusion.2 = bf16[1536,1280]{1,0:T(8,128)(2,1)} fusion(bf16[2048,1664]{1,0:T(8,128)(2,1)} %shard_map.448, bf16[2048,2560]{1,0:T(8,128)(2,1)} %shard_map.449), kind=kOutput, calls=%fused_computation.15 | convolution fusion | flops 8055029760 | bytes 15466496 | tf_op jit(solution)/shard_map/dot_general | solution.py:95
  429.8 10.0 %convolution_convert_fusion.3.a_ref = bf16[1536,1280]{1,0:T(8,128)(2,1)} fusion(bf16[2048,1664]{1,0:T(8,128)(2,1)S(1)} %copy-done.6, bf16[2048,2560]{1,0:T(8,128)(2,1)S(1)} %bitcast.187), kind=kOutput, calls=%fused_computation.16 | convolution fusion | flops 8055029760 | bytes 15466496 | tf_op jit(solution)/shard_map/dot_general | solution.py:95
  441.5 7.6 fusion.54
  455.0 7.0 add_convert_fusion.refs_0_
  470.0 8.2 %convolution_convert_fusion.6 = bf16[640,1536]{1,0:T(8,128)(2,1)S(1)} fusion(bf16[2048,1536]{1,0:T(8,128)(2,1)} %constant_dynamic-update-slice_fusion.11.refs_1_, bf16[2048,1280]{1,0:T(8,128)(2,1)} %shard_map.446), kind=kOutput, calls=%fused_computation.41 | convolution fusion | flops 4027514880 | bytes 10878976 | tf_op jit(solution)/shard_map/dot_general | solution.py:95
  478.9 7.1 convolution_convert_fusion.7.b_ref.c_ref
  486.0 18.6 %collective-permute-done.25 = bf16[2,256,1536]{2,1,0:T(8,128)(2,1)S(1)} collective-permute-done((bf16[2,256,1536]{2,1,0:T(8,128)(2,1)S(1)}, bf16[2,256,1536]{2,1,0:T(8,128)(2,1)S(1)}, u32[]{:S(2)}, u32[]{:S(2)}) %collective-permute-start.25) | collective-permute-done | bytes 1572896 | tf_op jit(solution)/shard_map/ppermute | solution.py:151
  506.1 9.0 %collective-permute-done.31 = bf16[2,256,1536]{2,1,0:T(8,128)(2,1)S(1)} collective-permute-done((bf16[2,256,1536]{2,1,0:T(8,128)(2,1)S(1)}, bf16[2,256,1536]{2,1,0:T(8,128)(2,1)S(1)}, u32[]{:S(2)}, u32[]{:S(2)}) %collective-permute-start.31) | collective-permute-done | bytes 1572896 | tf_op jit(solution)/shard_map/ppermute | solution.py:151
  516.7 8.2 %shard_map.450 = (bf16[8,192,1024]{2,1,0:T(8,128)(2,1)}, bf16[8,192,768]{2,1,0:T(8,128)(2,1)}, f32[128,1536]{1,0:T(8,128)S(1)}) custom-call(bf16[1536,1280]{1,0:T(8,128)(2,1)} %convolution_convert_fusion.3.a_ref, bf16[1536,1280]{1,0:T(8,128)(2,1)} %collective-permute-done.26.came_a_ref, bf16[640,1536]{1,0:T(8,128)(2,1)S(1)} %convolution_convert_fusion.7.b_ref.c_ref, ...), custom_call_target="tpu_custom_call" | custom-call | bytes 16777216 | tf_op jit(solution)/shard_map/pallas_call | solution.py:425
  585.3 12.1 %collective-permute-done.30 = bf16[384,768]{1,0:T(8,128)(2,1)S(1)} collective-permute-done((bf16[384,768]{1,0:T(8,128)(2,1)S(1)}, bf16[384,768]{1,0:T(8,128)(2,1)S(1)}, u32[]{:S(2)}, u32[]{:S(2)}) %collective-permute-start.30) | collective-permute-done | bytes 589856 | tf_op jit(solution)/shard_map/ppermute | solution.py:151
  605.1 8.3 %all-to-all-start.2 = ((bf16[8,192,768]{2,1,0:T(8,128)(2,1)}), bf16[8,192,768]{2,1,0:T(8,128)(2,1)S(1)}, u32[]{:S(2)}, u32[]{:S(2)}) async-start(bf16[8,192,768]{2,1,0:T(8,128)(2,1)} %shard_map.456), calls=%async_computation.2 | async-start | bytes 4718592 | tf_op jit(solution)/shard_map/all_to_all | solution.py:334
  627.8 25.3 %collective-permute-done.33 = bf16[2,384,1408]{2,1,0:T(8,128)(2,1)S(1)} collective-permute-done((bf16[2,384,1408]{2,1,0:T(8,128)(2,1)S(1)}, bf16[2,384,1408]{2,1,0:T(8,128)(2,1)S(1)}, u32[]{:S(2)}, u32[]{:S(2)}) %collective-permute-start.33) | collective-permute-done | bytes 2162720 | tf_op jit(solution)/shard_map/ppermute | solution.py:151
  670.0 13.6 %shard_map.460 = (f32[10,64,1536]{2,1,0:T(8,128)}, f32[10,64,1536]{2,1,0:T(8,128)}, f32[10,64,1536]{2,1,0:T(8,128)}) custom-call(bf16[8,192,768]{2,1,0:T(8,128)(2,1)S(1)} %all-to-all-done.2.refs_1_.home_ref, f32[128,1536]{1,0:T(8,128)S(1)} %copy-done.8, f32[10,64,1536]{2,1,0:T(8,128)} %w_ref.5, f32[10,64,1536]{2,1,0:T(8,128)} %m_ref.5, f32[10,64,1536]{2,1,0:T(8,128)} %s_ref.5), custom_call_target="tpu_custom_call" | custom-call | bytes 16777216 | tf_op jit(solution)/shard_map/pallas_call | solution.py:528
  683.6 16.0 %shard_map.458 = (f32[10,192,1024]{2,1,0:T(8,128)}, f32[10,192,1024]{2,1,0:T(8,128)}, f32[10,192,1024]{2,1,0:T(8,128)}) custom-call(bf16[8,192,1024]{2,1,0:T(8,128)(2,1)S(1)} %copy-done.4, f32[10,192,1024]{2,1,0:T(8,128)} %w_ref.4, f32[10,192,1024]{2,1,0:T(8,128)} %m_ref.4, f32[10,192,1024]{2,1,0:T(8,128)} %s_ref.4), custom_call_target="tpu_custom_call" | custom-call | bytes 33554432 | tf_op jit(solution)/shard_map/pallas_call | solution.py:507
  710.2 9.0 %collective-permute-done.35 = bf16[1,256,1536]{2,1,0:T(8,128)(2,1)S(1)} collective-permute-done((bf16[1,256,1536]{2,1,0:T(8,128)(2,1)S(1)}, bf16[1,256,1536]{2,1,0:T(8,128)(2,1)S(1)}, u32[]{:S(2)}, u32[]{:S(2)}) %collective-permute-start.35) | collective-permute-done | bytes 786464 | tf_op jit(solution)/shard_map/ppermute | solution.py:151
  753.4 24.5 %collective-permute-start.43 = (bf16[48,2176]{1,0:T(8,128)(2,1)S(1)}, bf16[48,2176]{1,0:T(8,128)(2,1)S(1)}, u32[]{:S(2)}, u32[]{:S(2)}) collective-permute-start(bf16[48,2176]{1,0:T(8,128)(2,1)S(1)} %broadcast_select_fusion), channel_id=1, source_target_pairs={{0,1},{1,0},{2,3},{3,2},{4,5},{5,4},{6,7},{7,6},{8,9},{9,8},{10,11... | collective-permute-start | bytes 626696 | tf_op jit(solution)/shard_map/ppermute | solution.py:104
  (585 shorter events, 291.9 us)
Async XLA Ops:
  7.2 107.3 %all-gather.3.cloned.1.call-start = ((), (), s32[]{:S(2)}) async-start(), calls=%async_computation.3 | async-start | bytes 8515584 | tf_op jit(solution)/shard_map/all_gather | solution.py:667
  67.1 46.4 %collective-permute-start.5 = (bf16[768,768]{1,0:T(8,128)(2,1)}, bf16[768,768]{1,0:T(8,128)(2,1)S(1)}, u32[]{:S(2)}, u32[]{:S(2)}) collective-permute-start(bf16[768,768]{1,0:T(8,128)(2,1)} %get-tuple-element.205), channel_id=1, source_target_pairs={{0,2},{1,5},{2,0},{3,7},{4,6},{5,1},{6,4},{7,3},{8,10},{9,13},{10,... | collective-permute-start | bytes 3538952 | tf_op jit(solution)/shard_map/ppermute | solution.py:151
  68.2 23.2 %collective-permute-start.8 = (bf16[128,1536]{1,0:T(8,128)(2,1)S(1)}, bf16[128,1536]{1,0:T(8,128)(2,1)S(1)}, u32[]{:S(2)}, u32[]{:S(2)}) collective-permute-start(bf16[128,1536]{1,0:T(8,128)(2,1)S(1)} %collective-permute-done.7), channel_id=1, source_target_pairs={{0,8},{1,9},{2,10},{3,11},{4,12},{5,13},{6,14},{7,15},{8,24},{9,25... | collective-permute-start | bytes 1179656 | tf_op jit(solution)/shard_map/ppermute | solution.py:151
  107.7 152.9 %all-to-all-start = ((bf16[8,192,1792]{2,1,0:T(8,128)(2,1)}), bf16[8,192,1792]{2,1,0:T(8,128)(2,1)}, u32[]{:S(2)}, u32[]{:S(2)}) async-start(bf16[8,192,1792]{2,1,0:T(8,128)(2,1)} %shard_map.442), calls=%async_computation | async-start | bytes 11010048 | tf_op jit(solution)/shard_map/all_to_all | solution.py:334
  112.9 197.9 %all-gather.5.cloned.1.call-start = ((), (), s32[]{:S(2)}) async-start(), calls=%async_computation.4 | async-start | bytes 7241728 | tf_op jit(solution)/shard_map/all_gather | solution.py:737
  114.6 18.1 %collective-permute-start.6 = (bf16[1536,768]{1,0:T(8,128)(2,1)}, bf16[1536,768]{1,0:T(8,128)(2,1)}, u32[]{:S(2)}, u32[]{:S(2)}) collective-permute-start(bf16[1536,768]{1,0:T(8,128)(2,1)} %constant_dynamic-update-slice_fusion.5), channel_id=1, source_target_pairs={{0,1},{1,0},{2,3},{3,2},{4,5},{5,4},{6,7},{7,6},{8,9},{9,8},{10,11... | collective-permute-start | bytes 7077896 | tf_op jit(solution)/shard_map/ppermute | solution.py:104
  140.4 37.3 %collective-permute-start.10 = (bf16[256,1536]{1,0:T(8,128)(2,1)}, bf16[256,1536]{1,0:T(8,128)(2,1)S(1)}, u32[]{:S(2)}, u32[]{:S(2)}) collective-permute-start(bf16[256,1536]{1,0:T(8,128)(2,1)} %shard_map.440), channel_id=1, source_target_pairs={{0,4},{1,5},{2,6},{3,7},{4,0},{5,1},{6,2},{7,3},{8,12},{9,13},{10,... | collective-permute-start | bytes 2359304 | tf_op jit(solution)/shard_map/ppermute | solution.py:151
  143.3 37.0 %collective-permute-start.12 = (bf16[256,1536]{1,0:T(8,128)(2,1)}, bf16[256,1536]{1,0:T(8,128)(2,1)S(1)}, u32[]{:S(2)}, u32[]{:S(2)}) collective-permute-start(bf16[256,1536]{1,0:T(8,128)(2,1)} %shard_map.441), channel_id=1, source_target_pairs={{0,2},{1,3},{2,0},{3,1},{4,6},{5,7},{6,4},{7,5},{8,10},{9,11},{10,... | collective-permute-start | bytes 2359304 | tf_op jit(solution)/shard_map/ppermute | solution.py:151
  177.8 35.6 %collective-permute-start.11 = (bf16[512,1536]{1,0:T(8,128)(2,1)S(1)}, bf16[512,1536]{1,0:T(8,128)(2,1)S(1)}, u32[]{:S(2)}, u32[]{:S(2)}) collective-permute-start(bf16[512,1536]{1,0:T(8,128)(2,1)S(1)} %pad_maximum_fusion.2), channel_id=1, source_target_pairs={{0,2},{1,3},{2,0},{3,1},{4,6},{5,7},{6,4},{7,5},{8,10},{9,11},{10,... | collective-permute-start | bytes 4718600 | tf_op jit(solution)/shard_map/ppermute | solution.py:151
  180.4 62.3 %collective-permute-start.13 = (bf16[512,1536]{1,0:T(8,128)(2,1)S(1)}, bf16[512,1536]{1,0:T(8,128)(2,1)S(1)}, u32[]{:S(2)}, u32[]{:S(2)}) collective-permute-start(bf16[512,1536]{1,0:T(8,128)(2,1)S(1)} %pad_maximum_fusion.3), channel_id=1, source_target_pairs={{0,4},{1,5},{2,6},{3,7},{4,0},{5,1},{6,2},{7,3},{8,12},{9,13},{10,... | collective-permute-start | bytes 4718600 | tf_op jit(solution)/shard_map/ppermute | solution.py:151
  260.6 16.5 %collective-permute-start.14 = (bf16[1536,1792]{1,0:T(8,128)(2,1)}, bf16[1536,1792]{1,0:T(8,128)(2,1)}, u32[]{:S(2)}, u32[]{:S(2)}) collective-permute-start(bf16[1536,1792]{1,0:T(8,128)(2,1)} %shard_map.443.refs_4_), channel_id=1, source_target_pairs={{0,1},{1,0},{2,3},{3,2},{4,5},{5,4},{6,7},{7,6},{8,9},{9,8},{10,11... | collective-permute-start | bytes 16515080 | tf_op jit(solution)/shard_map/ppermute | solution.py:104
  261.6 19.1 %collective-permute-start.15 = (bf16[128,1536]{1,0:T(8,128)(2,1)S(1)}, bf16[128,1536]{1,0:T(8,128)(2,1)S(1)}, u32[]{:S(2)}, u32[]{:S(2)}) collective-permute-start(bf16[128,1536]{1,0:T(8,128)(2,1)S(1)} %copy-done.10), channel_id=1, source_target_pairs={{0,1},{1,0},{2,3},{3,2},{4,5},{5,4},{6,7},{7,6},{8,9},{9,8},{10,11... | collective-permute-start | bytes 1179656 | tf_op jit(solution)/shard_map/ppermute | solution.py:104
  348.5 34.5 %collective-permute-start.18 = (bf16[2,128,1664]{2,1,0:T(8,128)(2,1)}, bf16[2,128,1664]{2,1,0:T(8,128)(2,1)S(1)}, u32[]{:S(2)}, u32[]{:S(2)}) collective-permute-start(bf16[2,128,1664]{2,1,0:T(8,128)(2,1)} %get-tuple-element.173), channel_id=1, source_target_pairs={{0,2},{1,3},{2,0},{3,1},{4,6},{5,7},{6,4},{7,5},{8,10},{9,11},{10,... | collective-permute-start | bytes 2555912 | tf_op jit(solution)/shard_map/ppermute | solution.py:151
  350.0 33.0 %collective-permute-start.20 = (bf16[2,128,1664]{2,1,0:T(8,128)(2,1)S(1)}, bf16[2,128,1664]{2,1,0:T(8,128)(2,1)S(1)}, u32[]{:S(2)}, u32[]{:S(2)}) collective-permute-start(bf16[2,128,1664]{2,1,0:T(8,128)(2,1)S(1)} %get-tuple-element.174), channel_id=1, source_target_pairs={{0,4},{1,5},{2,6},{3,7},{4,0},{5,1},{6,2},{7,3},{8,12},{9,13},{10,... | collective-permute-start | bytes 2555912 | tf_op jit(solution)/shard_map/ppermute | solution.py:151
  380.9 18.7 %collective-permute-start.16 = (bf16[2,128,1664]{2,1,0:T(8,128)(2,1)S(1)}, bf16[2,128,1664]{2,1,0:T(8,128)(2,1)S(1)}, u32[]{:S(2)}, u32[]{:S(2)}) collective-permute-start(bf16[2,128,1664]{2,1,0:T(8,128)(2,1)S(1)} %get-tuple-element.178), channel_id=1, source_target_pairs={{0,2},{1,3},{2,0},{3,1},{4,6},{5,7},{6,4},{7,5},{8,10},{9,11},{10,... | collective-permute-start | bytes 2555912 | tf_op jit(solution)/shard_map/ppermute | solution.py:151
  381.4 18.9 %collective-permute-start.17 = (bf16[2,128,1664]{2,1,0:T(8,128)(2,1)S(1)}, bf16[2,128,1664]{2,1,0:T(8,128)(2,1)S(1)}, u32[]{:S(2)}, u32[]{:S(2)}) collective-permute-start(bf16[2,128,1664]{2,1,0:T(8,128)(2,1)S(1)} %get-tuple-element.177), channel_id=1, source_target_pairs={{0,4},{1,5},{2,6},{3,7},{4,0},{5,1},{6,2},{7,3},{8,12},{9,13},{10,... | collective-permute-start | bytes 2555912 | tf_op jit(solution)/shard_map/ppermute | solution.py:151
  401.9 18.3 %collective-permute-start.19 = (bf16[1,256,1664]{2,1,0:T(8,128)(2,1)}, bf16[1,256,1664]{2,1,0:T(8,128)(2,1)}, u32[]{:S(2)}, u32[]{:S(2)}) collective-permute-start(bf16[1,256,1664]{2,1,0:T(8,128)(2,1)} %fusion.69), channel_id=1, source_target_pairs={{0,4},{1,5},{2,6},{3,7},{4,0},{5,1},{6,2},{7,3},{8,12},{9,13},{10,... | collective-permute-start | bytes 2555912 | tf_op jit(solution)/shard_map/ppermute | solution.py:151
  404.1 18.2 %collective-permute-start.21 = (bf16[1,256,1664]{2,1,0:T(8,128)(2,1)}, bf16[1,256,1664]{2,1,0:T(8,128)(2,1)}, u32[]{:S(2)}, u32[]{:S(2)}) collective-permute-start(bf16[1,256,1664]{2,1,0:T(8,128)(2,1)} %fusion.68), channel_id=1, source_target_pairs={{0,2},{1,3},{2,0},{3,1},{4,6},{5,7},{6,4},{7,5},{8,10},{9,11},{10,... | collective-permute-start | bytes 2555912 | tf_op jit(solution)/shard_map/ppermute | solution.py:151
  439.8 76.9 %collective-permute-start.26 = (bf16[1536,1280]{1,0:T(8,128)(2,1)}, bf16[1536,1280]{1,0:T(8,128)(2,1)}, u32[]{:S(2)}, u32[]{:S(2)}) collective-permute-start(bf16[1536,1280]{1,0:T(8,128)(2,1)} %convolution_convert_fusion.2), channel_id=1, source_target_pairs={{0,1},{1,0},{2,3},{3,2},{4,5},{5,4},{6,7},{7,6},{8,9},{9,8},{10,11... | collective-permute-start | bytes 11796488 | tf_op jit(solution)/shard_map/ppermute | solution.py:104
  469.4 35.2 %collective-permute-start.25 = (bf16[2,256,1536]{2,1,0:T(8,128)(2,1)S(1)}, bf16[2,256,1536]{2,1,0:T(8,128)(2,1)S(1)}, u32[]{:S(2)}, u32[]{:S(2)}) collective-permute-start(bf16[2,256,1536]{2,1,0:T(8,128)(2,1)S(1)} %bitcast.207), channel_id=1, source_target_pairs={{0,2},{1,3},{2,0},{3,1},{4,6},{5,7},{6,4},{7,5},{8,10},{9,11},{10,... | collective-permute-start | bytes 4718600 | tf_op jit(solution)/shard_map/ppermute | solution.py:151
  478.2 38.5 %collective-permute-start.27 = (bf16[640,1536]{1,0:T(8,128)(2,1)S(1)}, bf16[640,1536]{1,0:T(8,128)(2,1)S(1)}, u32[]{:S(2)}, u32[]{:S(2)}) collective-permute-start(bf16[640,1536]{1,0:T(8,128)(2,1)S(1)} %convolution_convert_fusion.6), channel_id=1, source_target_pairs={{0,1},{1,0},{2,3},{3,2},{4,5},{5,4},{6,7},{7,6},{8,9},{9,8},{10,11... | collective-permute-start | bytes 5898248 | tf_op jit(solution)/shard_map/ppermute | solution.py:104
  478.3 36.8 %collective-permute-start.31 = (bf16[2,256,1536]{2,1,0:T(8,128)(2,1)S(1)}, bf16[2,256,1536]{2,1,0:T(8,128)(2,1)S(1)}, u32[]{:S(2)}, u32[]{:S(2)}) collective-permute-start(bf16[2,256,1536]{2,1,0:T(8,128)(2,1)S(1)} %bitcast.206), channel_id=1, source_target_pairs={{0,4},{1,5},{2,6},{3,7},{4,0},{5,1},{6,2},{7,3},{8,12},{9,13},{10,... | collective-permute-start | bytes 4718600 | tf_op jit(solution)/shard_map/ppermute | solution.py:151
  525.9 74.9 %all-to-all-start.1 = ((bf16[8,192,1024]{2,1,0:T(8,128)(2,1)}), bf16[8,192,1024]{2,1,0:T(8,128)(2,1)S(1)}, u32[]{:S(2)}, u32[]{:S(2)}) async-start(bf16[8,192,1024]{2,1,0:T(8,128)(2,1)} %shard_map.452), calls=%async_computation.1 | async-start | bytes 6291456 | tf_op jit(solution)/shard_map/all_to_all | solution.py:334
  538.6 18.2 %collective-permute-start.28 = (bf16[1536,768]{1,0:T(8,128)(2,1)}, bf16[1536,768]{1,0:T(8,128)(2,1)}, u32[]{:S(2)}, u32[]{:S(2)}) collective-permute-start(bf16[1536,768]{1,0:T(8,128)(2,1)} %convolution_convert_fusion.5), channel_id=1, source_target_pairs={{0,1},{1,0},{2,3},{3,2},{4,5},{5,4},{6,7},{7,6},{8,9},{9,8},{10,11... | collective-permute-start | bytes 7077896 | tf_op jit(solution)/shard_map/ppermute | solution.py:104
  562.2 16.5 %collective-permute-start.29 = (bf16[2,384,768]{2,1,0:T(8,128)(2,1)}, bf16[2,384,768]{2,1,0:T(8,128)(2,1)}, u32[]{:S(2)}, u32[]{:S(2)}) collective-permute-start(bf16[2,384,768]{2,1,0:T(8,128)(2,1)} %bitcast.53), channel_id=1, source_target_pairs={{0,2},{1,5},{2,0},{3,7},{4,6},{5,1},{6,4},{7,3},{8,10},{9,13},{10,... | collective-permute-start | bytes 3538952 | tf_op jit(solution)/shard_map/ppermute | solution.py:151
  580.8 16.5 %collective-permute-start.30 = (bf16[384,768]{1,0:T(8,128)(2,1)S(1)}, bf16[384,768]{1,0:T(8,128)(2,1)S(1)}, u32[]{:S(2)}, u32[]{:S(2)}) collective-permute-start(bf16[384,768]{1,0:T(8,128)(2,1)S(1)} %slice_bitcast_fusion.3), channel_id=1, source_target_pairs={{0,4},{1,3},{2,6},{3,1},{4,0},{5,7},{6,2},{7,5},{8,12},{9,11},{10,... | collective-permute-start | bytes 1769480 | tf_op jit(solution)/shard_map/ppermute | solution.py:151
  602.4 19.6 %collective-permute-start.32 = (bf16[1536,1408]{1,0:T(8,128)(2,1)}, bf16[1536,1408]{1,0:T(8,128)(2,1)}, u32[]{:S(2)}, u32[]{:S(2)}) collective-permute-start(bf16[1536,1408]{1,0:T(8,128)(2,1)} %shard_map.453), channel_id=1, source_target_pairs={{0,1},{1,0},{2,3},{3,2},{4,5},{5,4},{6,7},{7,6},{8,9},{9,8},{10,11... | collective-permute-start | bytes 12976136 | tf_op jit(solution)/shard_map/ppermute | solution.py:104
  605.1 64.8 %all-to-all-start.2 = ((bf16[8,192,768]{2,1,0:T(8,128)(2,1)}), bf16[8,192,768]{2,1,0:T(8,128)(2,1)S(1)}, u32[]{:S(2)}, u32[]{:S(2)}) async-start(bf16[8,192,768]{2,1,0:T(8,128)(2,1)} %shard_map.456), calls=%async_computation.2 | async-start | bytes 4718592 | tf_op jit(solution)/shard_map/all_to_all | solution.py:334
  626.3 26.8 %collective-permute-start.33 = (bf16[2,384,1408]{2,1,0:T(8,128)(2,1)S(1)}, bf16[2,384,1408]{2,1,0:T(8,128)(2,1)S(1)}, u32[]{:S(2)}, u32[]{:S(2)}) collective-permute-start(bf16[2,384,1408]{2,1,0:T(8,128)(2,1)S(1)} %bitcast.205), channel_id=1, source_target_pairs={{0,2},{1,5},{2,0},{3,7},{4,6},{5,1},{6,4},{7,3},{8,10},{9,13},{10,... | collective-permute-start | bytes 6488072 | tf_op jit(solution)/shard_map/ppermute | solution.py:151
  657.2 50.9 %collective-permute-start.34 = (bf16[1,256,1536]{2,1,0:T(8,128)(2,1)}, bf16[1,256,1536]{2,1,0:T(8,128)(2,1)}, u32[]{:S(2)}, u32[]{:S(2)}) collective-permute-start(bf16[1,256,1536]{2,1,0:T(8,128)(2,1)} %slice.555), channel_id=1, source_target_pairs={{0,4},{1,5},{2,6},{3,7},{4,0},{5,1},{6,2},{7,3},{8,12},{9,13},{10,... | collective-permute-start | bytes 2359304 | tf_op jit(solution)/shard_map/ppermute | solution.py:151
  745.2 32.6 %collective-permute-start.38 = (bf16[128,1536]{1,0:T(8,128)(2,1)S(1)}, bf16[128,1536]{1,0:T(8,128)(2,1)S(1)}, u32[]{:S(2)}, u32[]{:S(2)}) collective-permute-start(bf16[128,1536]{1,0:T(8,128)(2,1)S(1)} %add_convert_fusion.19), channel_id=1, source_target_pairs={{0,16},{1,17},{2,18},{3,19},{4,20},{5,21},{6,22},{7,23},{8,0},{9,1... | collective-permute-start | bytes 1179656 | tf_op jit(solution)/shard_map/ppermute | solution.py:151
  753.4 26.2 %collective-permute-start.43 = (bf16[48,2176]{1,0:T(8,128)(2,1)S(1)}, bf16[48,2176]{1,0:T(8,128)(2,1)S(1)}, u32[]{:S(2)}, u32[]{:S(2)}) collective-permute-start(bf16[48,2176]{1,0:T(8,128)(2,1)S(1)} %broadcast_select_fusion), channel_id=1, source_target_pairs={{0,1},{1,0},{2,3},{3,2},{4,5},{5,4},{6,7},{7,6},{8,9},{9,8},{10,11... | collective-permute-start | bytes 626696 | tf_op jit(solution)/shard_map/ppermute | solution.py:104
  (158 other events, 1543.0 us)
Sparse Core Ops, SparseCore 0:
  11.6 96.6 all-gather.2
  139.4 171.4 all-gather.4

commit v2 on v1

--- a/solution.py
+++ b/solution.py
@@ -759,8 +759,7 @@
         gated, grad_both = after(gated, *firsts[-1], always=True), after(grad_both, *firsts[-1])
         rows_all = after(sent_all, *firsts[-1], always=True)[:, :D]
         mixed = (dot(gated[:, :units], down_own) + dot(gated[:, units:], down_other)).astype(bf16)
-        mixed = after(mixed, two_sum, always=True).reshape(blocks, -1, D)
-        mixed_first = scatter_first(mixed)
+        mixed = after(mixed, two_sum, always=True)
 
         came_gate_up = swap_core(dot_tn(rows_all, grad_both[:, 2 * units :]).astype(bf16))
         came_down = swap_core(dot_tn(gated[:, units:], cot_all).astype(bf16))
@@ -842,17 +841,16 @@
             product = dot_tn(hidden, jnp.where(at == 0, joined_left, joined_right))
             extra = jnp.where(at == 0, dot_tn(rows_order, small_sent), 0.0)
             qkv_sent.append(jnp.concatenate([product, extra], axis=1).astype(bf16))
-        qkv_first = scatter_halves_first(qkv_sent[0], after(qkv_sent[1], out_two, home_full, *mixed_first))
-        mixed = sum_line(scatter_second([[after(m, qkv_first) for m in mixed_first]]))
+        qkv_first = scatter_halves_first(qkv_sent[0], after(qkv_sent[1], out_two, home_full))
+        mixed = after(mixed, qkv_first).reshape(blocks, -1, D)
+        mixed = sum_line(scatter_second([scatter_first(mixed)]))
         layer_out = (mid + residual_scale * mixed).astype(bf16)
+        qkv_two = scatter_halves_second(qkv_first)
+        if whole:
+            home_full = after(home_full, qkv_two)
         (out_left, out_right), (qkv_left, qkv_right) = scatter_halves_line(
-            [out_two, scatter_halves_second(qkv_first)], home_rest
-        )
-        sum_out = jnp.concatenate([out_left, out_right], axis=1)
-        sum_qkv = jnp.concatenate([qkv_left[:, : QKV // 2], qkv_right[:, : QKV // 2]], axis=1)
-        sum_router = qkv_left[:, QKV // 2 : QKV // 2 + EXPERTS]
-        sum_gains = qkv_left[:, QKV // 2 + EXPERTS : QKV // 2 + EXPERTS + 2].T
-
+            [out_two, qkv_two], home_rest
+        )
         new_gate_up, new_down = update_experts(
             home_full,
             home_rest,
@@ -860,6 +858,11 @@
             (weight_gate_up, moment_gate_up, square_gate_up),
             (weight_down, moment_down, square_down),
         )
+        sum_out = jnp.concatenate([out_left, out_right], axis=1)
+        sum_qkv = jnp.concatenate([qkv_left[:, : QKV // 2], qkv_right[:, : QKV // 2]], axis=1)
+        sum_router = qkv_left[:, QKV // 2 : QKV // 2 + EXPERTS]
+        sum_gains = qkv_left[:, QKV // 2 + EXPERTS : QKV // 2 + EXPERTS + 2].T
+
         new_qkv = adam_step(weight_qkv, moment_qkv, square_qkv, sum_qkv, D ** (-0.5), weight_decay)
         new_out = adam_step(
             weight_out,

time: 805 us -> 783 us (0.973)
  starting transfers between devices: 100 us -> 78.5 us
    ppermute x9, starting transfers between devices: 27.8 us -> 13.5 us  [swap_core(): return lax.ppermute(values, 'core', [(0, 1), (1, 0)])]
    ppermute x35, starting transfers between devices: 53.7 us -> 45.4 us  [move(): return lax.ppermute(values, ALL, pairs_of(axes, step))]
    unnamed x307 -> x305, local copies, waits for them, and re-layouts: 44.6 us -> 49.2 us
  transfers between devices with their start and end apart: 49 -> 49, of which waited for: 29 -> 26; matrix products, arithmetic and copies ran while one was open for 27% -> 29% of each run, Pallas kernels for 9% -> 5%
where the time goes in v2:
time: 783 us; the launch traced here: 778 us
  waiting for transfers between devices  309 us (39%)
  matrix products  131 us (17%)
  Pallas kernels  108 us (14%)
  local copies, waits for them, and re-layouts  83 us (11%)
  starting transfers between devices  78.5 us (10%)
  other arithmetic  51.8 us (7%)
  between operations  16.3 us (2%)
    ppermute x35, waiting for transfers between devices, move(): return lax.ppermute(values, ALL, pairs_of(axes, step))  270 us
    dot_general x11, matrix products, dot_tn(): lax.dot_general(a, b, (((0,), (0,)), ((), ())), preferred_element_type=f32)  64.6 us
    pallas_call x2, Pallas kernels, run_experts(): pl.pallas_call(functools.partial(expert_kernel, not kept), grid=(blocks /...  56.7 us
    unnamed x305, local copies, waits for them, and re-layouts  49.2 us
    ppermute x35, starting transfers between devices, move(): return lax.ppermute(values, ALL, pairs_of(axes, step))  45.4 us
    dot_general x6, matrix products, dot_nt(): lax.dot_general(a, b, (((1,), (1,)), ((), ())), preferred_element_type=f32)  36.1 us
    dot_general x8, matrix products, dot(): return jnp.dot(a, b, preferred_element_type=f32)  26.3 us
    convert_element_type x20, other arithmetic, add_low(): return (a.astype(f32) + b.astype(f32)).astype(bf16)  20.5 us
  transfers between devices with their start and end apart: 49, of which 26 were waited for; matrix products, arithmetic and copies ran while one was open for 29% of the time, Pallas kernels for 5%

profile of v2, /device:TPU:0, one launch (start us, length us, event | category | flops | bytes accessed | tf_op | source)
XLA Modules:
  0.0 778.3 jit_solution(11587000842052420490)
XLA Ops:
  15.3 8.5 %shard_map.438 = (bf16[8,192,1792]{2,1,0:T(8,128)(2,1)}, bf16[128,1536]{1,0:T(8,128)(2,1)S(1)}) custom-call(f32[10,192,1024]{2,1,0:T(8,128)} %w_ref.4, f32[10,192,1024]{2,1,0:T(8,128)} %w_ref.4, f32[10,64,1536]{2,1,0:T(8,128)S(1)} %copy-done.6, f32[10,64,1536]{2,1,0:T(8,128)S(1)} %copy-done.6), custom_call_target="tpu_custom_call" | custom-call | bytes 16777216 | tf_op jit(solution)/shard_map/pallas_call | solution.py:381
  28.0 8.3 %collective-permute-done.1.refs_2_ = bf16[96,768]{1,0:T(8,128)(2,1)S(1)} collective-permute-done((bf16[96,768]{1,0:T(8,128)(2,1)S(1)}, bf16[96,768]{1,0:T(8,128)(2,1)S(1)}, u32[]{:S(2)}, u32[]{:S(2)}) %collective-permute-start.1) | collective-permute-done | bytes 147488 | tf_op jit(solution)/shard_map/ppermute | solution.py:151
  43.0 13.0 %collective-permute-done.3.refs_2_ = bf16[96,768]{1,0:T(8,128)(2,1)S(1)} collective-permute-done((bf16[96,768]{1,0:T(8,128)(2,1)S(1)}, bf16[96,768]{1,0:T(8,128)(2,1)S(1)}, u32[]{:S(2)}, u32[]{:S(2)}) %collective-permute-start.3) | collective-permute-done | bytes 147488 | tf_op jit(solution)/shard_map/ppermute | solution.py:151
  68.5 22.1 %collective-permute-done.8 = bf16[128,1536]{1,0:T(8,128)(2,1)S(1)} collective-permute-done((bf16[128,1536]{1,0:T(8,128)(2,1)S(1)}, bf16[128,1536]{1,0:T(8,128)(2,1)S(1)}, u32[]{:S(2)}, u32[]{:S(2)}) %collective-permute-start.8) | collective-permute-done | bytes 393248 | tf_op jit(solution)/shard_map/ppermute | solution.py:151
  91.7 15.2 %collective-permute-done.9.refs_1_ = bf16[128,1536]{1,0:T(8,128)(2,1)S(1)} collective-permute-done((bf16[128,1536]{1,0:T(8,128)(2,1)S(1)}, bf16[128,1536]{1,0:T(8,128)(2,1)S(1)}, u32[]{:S(2)}, u32[]{:S(2)}) %collective-permute-start.9) | collective-permute-done | bytes 393248 | tf_op jit(solution)/shard_map/ppermute | solution.py:151
  145.5 32.4 %collective-permute-done.10 = bf16[256,1536]{1,0:T(8,128)(2,1)S(1)} collective-permute-done((bf16[256,1536]{1,0:T(8,128)(2,1)}, bf16[256,1536]{1,0:T(8,128)(2,1)S(1)}, u32[]{:S(2)}, u32[]{:S(2)}) %collective-permute-start.10) | collective-permute-done | bytes 786464 | tf_op jit(solution)/shard_map/ppermute | solution.py:151
  184.7 28.7 %collective-permute-done.11 = bf16[512,1536]{1,0:T(8,128)(2,1)S(1)} collective-permute-done((bf16[512,1536]{1,0:T(8,128)(2,1)S(1)}, bf16[512,1536]{1,0:T(8,128)(2,1)S(1)}, u32[]{:S(2)}, u32[]{:S(2)}) %collective-permute-start.11) | collective-permute-done | bytes 1572896 | tf_op jit(solution)/shard_map/ppermute | solution.py:151
  216.5 26.6 %collective-permute-done.13 = bf16[512,1536]{1,0:T(8,128)(2,1)S(1)} collective-permute-done((bf16[512,1536]{1,0:T(8,128)(2,1)S(1)}, bf16[512,1536]{1,0:T(8,128)(2,1)S(1)}, u32[]{:S(2)}, u32[]{:S(2)}) %collective-permute-start.13) | collective-permute-done | bytes 1572896 | tf_op jit(solution)/shard_map/ppermute | solution.py:151
  244.4 16.4 %all-to-all-done = bf16[8,192,1792]{2,1,0:T(8,128)(2,1)} async-done(((bf16[8,192,1792]{2,1,0:T(8,128)(2,1)}), bf16[8,192,1792]{2,1,0:T(8,128)(2,1)}, u32[]{:S(2)}, u32[]{:S(2)}) %all-to-all-start) | async-done | bytes 5505056 | tf_op jit(solution)/shard_map/all_to_all | solution.py:334
  267.7 9.5 %fusion.162 = f32[2048,640]{1,0:T(8,128)} fusion(bf16[2048,1536]{1,0:T(8,128)(2,1)} %constant_dynamic-update-slice_fusion.11.refs_1_, bf16[640,1536]{1,0:T(8,128)(2,1)S(1)} %constant_dynamic-update-slice_fusion.17), kind=kOutput, calls=%fused_computation.352 | convolution fusion | flops 4026531840 | bytes 13500416 | tf_op jit(solution)/shard_map/dot_general | solution.py:91
  282.1 8.7 %fusion.163 = f32[2048,640]{1,0:T(8,128)} fusion(bf16[2048,1536]{1,0:T(8,128)(2,1)} %constant_dynamic-update-slice_fusion.11.refs_1_, bf16[640,1536]{1,0:T(8,128)(2,1)S(1)} %constant_dynamic-update-slice_fusion.19), kind=kOutput, calls=%fused_computation.353 | convolution fusion | flops 4026531840 | bytes 13500416 | tf_op jit(solution)/shard_map/dot_general | solution.py:91
  290.7 20.1 %all-gather.5.cloned.1.call-done = bf16[2048,1664]{1,0:T(8,128)(2,1)} async-done(((bf16[128,1664]{1,0:T(8,128)(2,1)}), bf16[2048,1664]{1,0:T(8,128)(2,1)}) %all-gather.5.cloned.1.call-update) | async-done | bytes 6815760 | tf_op jit(solution)/shard_map/all_gather | solution.py:737
  317.8 28.2 %shard_map.444 = (bf16[8,256,1280]{2,1,0:T(8,128)(2,1)}, bf16[8,256,2560]{2,1,0:T(8,128)(2,1)}, bf16[8,128,1664]{2,1,0:T(8,128)(2,1)}) custom-call(bf16[8,256,1664]{2,1,0:T(8,128)(2,1)} %bitcast.180, bf16[8,256,1664]{2,1,0:T(8,128)(2,1)} %bitcast.181, f32[8,256,640]{2,1,0:T(8,128)} %bitcast.217, f32[8,256,640]{2,1,0:T(8,128)} %bitcast.219, ...), custom_call_target="tpu_custom_call" | custom-call | flops 16106127360 | bytes 33554432 | tf_op jit(solution)/shard_map/pallas_call | solution.py:611
  346.1 28.5 %shard_map.445 = (bf16[8,256,1280]{2,1,0:T(8,128)(2,1)}, bf16[8,256,2560]{2,1,0:T(8,128)(2,1)}, bf16[8,128,1664]{2,1,0:T(8,128)(2,1)}) custom-call(bf16[8,256,1664]{2,1,0:T(8,128)(2,1)} %bitcast.182, bf16[8,256,1664]{2,1,0:T(8,128)(2,1)} %bitcast.183, f32[8,256,640]{2,1,0:T(8,128)} %bitcast.218, ...), custom_call_target="tpu_custom_call", output_to_operand_aliasing={{0}: (8, {}), {1}: (9, {})} | custom-call | flops 16106127360 | bytes 33554432 | tf_op jit(solution)/shard_map/pallas_call | solution.py:611
  380.6 17.6 %collective-permute-done.16 = bf16[2,128,1664]{2,1,0:T(8,128)(2,1)S(1)} collective-permute-done((bf16[2,128,1664]{2,1,0:T(8,128)(2,1)S(1)}, bf16[2,128,1664]{2,1,0:T(8,128)(2,1)S(1)}, u32[]{:S(2)}, u32[]{:S(2)}) %collective-permute-start.16) | collective-permute-done | bytes 852000 | tf_op jit(solution)/shard_map/ppermute | solution.py:151
  401.4 13.9 %convolution_convert_fusion.2 = bf16[1536,1280]{1,0:T(8,128)(2,1)} fusion(bf16[2048,1664]{1,0:T(8,128)(2,1)} %shard_map.448, bf16[2048,2560]{1,0:T(8,128)(2,1)} %shard_map.449), kind=kOutput, calls=%fused_computation.15 | convolution fusion | flops 8055029760 | bytes 15466496 | tf_op jit(solution)/shard_map/dot_general | solution.py:95
  415.3 10.4 %convolution_convert_fusion.3.a_ref = bf16[1536,1280]{1,0:T(8,128)(2,1)} fusion(bf16[2048,1664]{1,0:T(8,128)(2,1)S(1)} %copy-done.8, bf16[2048,2560]{1,0:T(8,128)(2,1)S(1)} %copy-done.27), kind=kOutput, calls=%fused_computation.16 | convolution fusion | flops 8055029760 | bytes 15466496 | tf_op jit(solution)/shard_map/dot_general | solution.py:95
  428.2 9.2 %convolution_convert_fusion.6 = bf16[640,1536]{1,0:T(8,128)(2,1)} fusion(bf16[2048,1536]{1,0:T(8,128)(2,1)} %constant_dynamic-update-slice_fusion.11.refs_1_, bf16[2048,1280]{1,0:T(8,128)(2,1)} %shard_map.446), kind=kOutput, calls=%fused_computation.41 | convolution fusion | flops 4027514880 | bytes 10878976 | tf_op jit(solution)/shard_map/dot_general | solution.py:95
  458.3 7.0 add_convert_fusion.refs_0_
  469.4 8.3 %convolution_convert_fusion.7.b_ref.c_ref = bf16[640,1536]{1,0:T(8,128)(2,1)} fusion(bf16[2048,1536]{1,0:T(8,128)(2,1)} %constant_dynamic-update-slice_fusion.11.refs_1_, bf16[2048,1280]{1,0:T(8,128)(2,1)S(1)} %copy-done.32), kind=kOutput, calls=%fused_computation.42 | convolution fusion | flops 4027514880 | bytes 10878976 | tf_op jit(solution)/shard_map/dot_general | solution.py:95
  480.3 8.2 %shard_map.450 = (bf16[8,192,1024]{2,1,0:T(8,128)(2,1)}, bf16[8,192,768]{2,1,0:T(8,128)(2,1)}, f32[128,1536]{1,0:T(8,128)S(1)}) custom-call(bf16[1536,1280]{1,0:T(8,128)(2,1)} %convolution_convert_fusion.3.a_ref, bf16[1536,1280]{1,0:T(8,128)(2,1)} %collective-permute-done.25.came_a_ref, bf16[640,1536]{1,0:T(8,128)(2,1)S(1)} %copy-done.9, ...), custom_call_target="tpu_custom_call" | custom-call | bytes 16777216 | tf_op jit(solution)/shard_map/pallas_call | solution.py:425
  548.2 9.8 %collective-permute-done.29 = bf16[384,768]{1,0:T(8,128)(2,1)S(1)} collective-permute-done((bf16[384,768]{1,0:T(8,128)(2,1)S(1)}, bf16[384,768]{1,0:T(8,128)(2,1)S(1)}, u32[]{:S(2)}, u32[]{:S(2)}) %collective-permute-start.29) | collective-permute-done | bytes 589856 | tf_op jit(solution)/shard_map/ppermute | solution.py:151
  580.8 9.6 %all-to-all-start.2 = ((bf16[8,192,768]{2,1,0:T(8,128)(2,1)}), bf16[8,192,768]{2,1,0:T(8,128)(2,1)S(1)}, u32[]{:S(2)}, u32[]{:S(2)}) async-start(bf16[8,192,768]{2,1,0:T(8,128)(2,1)} %shard_map.455), calls=%async_computation.2 | async-start | bytes 4718592 | tf_op jit(solution)/shard_map/all_to_all | solution.py:334
  590.4 15.7 %collective-permute-done.31 = bf16[2,384,1408]{2,1,0:T(8,128)(2,1)} collective-permute-done((bf16[2,384,1408]{2,1,0:T(8,128)(2,1)}, bf16[2,384,1408]{2,1,0:T(8,128)(2,1)}, u32[]{:S(2)}, u32[]{:S(2)}) %collective-permute-start.31) | collective-permute-done | bytes 2162720 | tf_op jit(solution)/shard_map/ppermute | solution.py:151
  621.1 21.0 %collective-permute-done.39 = bf16[384,1408]{1,0:T(8,128)(2,1)} collective-permute-done((bf16[384,1408]{1,0:T(8,128)(2,1)}, bf16[384,1408]{1,0:T(8,128)(2,1)}, u32[]{:S(2)}, u32[]{:S(2)}) %collective-permute-start.39) | collective-permute-done | bytes 1081376 | tf_op jit(solution)/shard_map/ppermute | solution.py:151
  656.3 12.8 %shard_map.460 = (f32[10,64,1536]{2,1,0:T(8,128)}, f32[10,64,1536]{2,1,0:T(8,128)}, f32[10,64,1536]{2,1,0:T(8,128)}) custom-call(bf16[8,192,768]{2,1,0:T(8,128)(2,1)S(1)} %copy-done.4, f32[128,1536]{1,0:T(8,128)S(1)} %copy-done.11, f32[10,64,1536]{2,1,0:T(8,128)} %w_ref.5, f32[10,64,1536]{2,1,0:T(8,128)} %m_ref.5, f32[10,64,1536]{2,1,0:T(8,128)} %s_ref.5), custom_call_target="tpu_custom_call" | custom-call | bytes 16777216 | tf_op jit(solution)/shard_map/pallas_call | solution.py:528
  671.7 16.2 %shard_map.458 = (f32[10,192,1024]{2,1,0:T(8,128)}, f32[10,192,1024]{2,1,0:T(8,128)}, f32[10,192,1024]{2,1,0:T(8,128)}) custom-call(bf16[8,192,1024]{2,1,0:T(8,128)(2,1)S(1)} %copy-done.2, f32[10,192,1024]{2,1,0:T(8,128)} %w_ref.4, f32[10,192,1024]{2,1,0:T(8,128)} %m_ref.4, f32[10,192,1024]{2,1,0:T(8,128)} %s_ref.4), custom_call_target="tpu_custom_call" | custom-call | bytes 33554432 | tf_op jit(solution)/shard_map/pallas_call | solution.py:507
  699.0 9.5 %collective-permute-done.41 = bf16[96,2176]{1,0:T(8,128)(2,1)S(1)} collective-permute-done((bf16[96,2176]{1,0:T(8,128)(2,1)S(1)}, bf16[96,2176]{1,0:T(8,128)(2,1)S(1)}, u32[]{:S(2)}, u32[]{:S(2)}) %collective-permute-start.41) | collective-permute-done | bytes 417824 | tf_op jit(solution)/shard_map/ppermute | solution.py:151
  712.3 7.2 collective-permute-done.42
  719.7 10.7 %collective-permute-start.43 = (bf16[48,2176]{1,0:T(8,128)(2,1)S(1)}, bf16[48,2176]{1,0:T(8,128)(2,1)S(1)}, u32[]{:S(2)}, u32[]{:S(2)}) collective-permute-start(bf16[48,2176]{1,0:T(8,128)(2,1)S(1)} %broadcast_select_fusion), channel_id=1, source_target_pairs={{0,1},{1,0},{2,3},{3,2},{4,5},{5,4},{6,7},{7,6},{8,9},{9,8},{10,11... | collective-permute-start | bytes 626696 | tf_op jit(solution)/shard_map/ppermute | solution.py:104
  746.8 10.0 %collective-permute-done.37 = bf16[128,1536]{1,0:T(8,128)(2,1)S(1)} collective-permute-done((bf16[128,1536]{1,0:T(8,128)(2,1)S(1)}, bf16[128,1536]{1,0:T(8,128)(2,1)S(1)}, u32[]{:S(2)}, u32[]{:S(2)}) %collective-permute-start.37) | collective-permute-done | bytes 393248 | tf_op jit(solution)/shard_map/ppermute | solution.py:151
  758.1 11.5 %collective-permute-done.38 = bf16[128,1536]{1,0:T(8,128)(2,1)S(1)} collective-permute-done((bf16[128,1536]{1,0:T(8,128)(2,1)S(1)}, bf16[128,1536]{1,0:T(8,128)(2,1)S(1)}, u32[]{:S(2)}, u32[]{:S(2)}) %collective-permute-start.38) | collective-permute-done | bytes 393248 | tf_op jit(solution)/shard_map/ppermute | solution.py:151
  (580 shorter events, 287.1 us)
Async XLA Ops:
  7.2 107.5 %all-gather.3.cloned.1.call-start = ((), (), s32[]{:S(2)}) async-start(), calls=%async_computation.3 | async-start | bytes 8515584 | tf_op jit(solution)/shard_map/all_gather | solution.py:667
  67.1 46.5 %collective-permute-start.5 = (bf16[768,768]{1,0:T(8,128)(2,1)}, bf16[768,768]{1,0:T(8,128)(2,1)S(1)}, u32[]{:S(2)}, u32[]{:S(2)}) collective-permute-start(bf16[768,768]{1,0:T(8,128)(2,1)} %get-tuple-element.205), channel_id=1, source_target_pairs={{0,2},{1,5},{2,0},{3,7},{4,6},{5,1},{6,4},{7,3},{8,10},{9,13},{10,... | collective-permute-start | bytes 3538952 | tf_op jit(solution)/shard_map/ppermute | solution.py:151
  68.2 22.3 %collective-permute-start.8 = (bf16[128,1536]{1,0:T(8,128)(2,1)S(1)}, bf16[128,1536]{1,0:T(8,128)(2,1)S(1)}, u32[]{:S(2)}, u32[]{:S(2)}) collective-permute-start(bf16[128,1536]{1,0:T(8,128)(2,1)S(1)} %collective-permute-done.7), channel_id=1, source_target_pairs={{0,8},{1,9},{2,10},{3,11},{4,12},{5,13},{6,14},{7,15},{8,24},{9,25... | collective-permute-start | bytes 1179656 | tf_op jit(solution)/shard_map/ppermute | solution.py:151
  90.6 16.3 %collective-permute-start.9 = (bf16[128,1536]{1,0:T(8,128)(2,1)S(1)}, bf16[128,1536]{1,0:T(8,128)(2,1)S(1)}, u32[]{:S(2)}, u32[]{:S(2)}) collective-permute-start(bf16[128,1536]{1,0:T(8,128)(2,1)S(1)} %collective-permute-done.8), channel_id=1, source_target_pairs={{0,8},{1,9},{2,10},{3,11},{4,12},{5,13},{6,14},{7,15},{8,24},{9,25... | collective-permute-start | bytes 1179656 | tf_op jit(solution)/shard_map/ppermute | solution.py:151
  107.6 153.2 %all-to-all-start = ((bf16[8,192,1792]{2,1,0:T(8,128)(2,1)}), bf16[8,192,1792]{2,1,0:T(8,128)(2,1)}, u32[]{:S(2)}, u32[]{:S(2)}) async-start(bf16[8,192,1792]{2,1,0:T(8,128)(2,1)} %shard_map.442), calls=%async_computation | async-start | bytes 11010048 | tf_op jit(solution)/shard_map/all_to_all | solution.py:334
  113.0 197.9 %all-gather.5.cloned.1.call-start = ((), (), s32[]{:S(2)}) async-start(), calls=%async_computation.4 | async-start | bytes 7241728 | tf_op jit(solution)/shard_map/all_gather | solution.py:737
  114.7 17.9 %collective-permute-start.6 = (bf16[1536,768]{1,0:T(8,128)(2,1)}, bf16[1536,768]{1,0:T(8,128)(2,1)}, u32[]{:S(2)}, u32[]{:S(2)}) collective-permute-start(bf16[1536,768]{1,0:T(8,128)(2,1)} %constant_dynamic-update-slice_fusion.5), channel_id=1, source_target_pairs={{0,1},{1,0},{2,3},{3,2},{4,5},{5,4},{6,7},{7,6},{8,9},{9,8},{10,11... | collective-permute-start | bytes 7077896 | tf_op jit(solution)/shard_map/ppermute | solution.py:104
  140.4 37.4 %collective-permute-start.10 = (bf16[256,1536]{1,0:T(8,128)(2,1)}, bf16[256,1536]{1,0:T(8,128)(2,1)S(1)}, u32[]{:S(2)}, u32[]{:S(2)}) collective-permute-start(bf16[256,1536]{1,0:T(8,128)(2,1)} %shard_map.440), channel_id=1, source_target_pairs={{0,4},{1,5},{2,6},{3,7},{4,0},{5,1},{6,2},{7,3},{8,12},{9,13},{10,... | collective-permute-start | bytes 2359304 | tf_op jit(solution)/shard_map/ppermute | solution.py:151
  143.3 37.0 %collective-permute-start.12 = (bf16[256,1536]{1,0:T(8,128)(2,1)}, bf16[256,1536]{1,0:T(8,128)(2,1)S(1)}, u32[]{:S(2)}, u32[]{:S(2)}) collective-permute-start(bf16[256,1536]{1,0:T(8,128)(2,1)} %shard_map.441), channel_id=1, source_target_pairs={{0,2},{1,3},{2,0},{3,1},{4,6},{5,7},{6,4},{7,5},{8,10},{9,11},{10,... | collective-permute-start | bytes 2359304 | tf_op jit(solution)/shard_map/ppermute | solution.py:151
  177.9 35.5 %collective-permute-start.11 = (bf16[512,1536]{1,0:T(8,128)(2,1)S(1)}, bf16[512,1536]{1,0:T(8,128)(2,1)S(1)}, u32[]{:S(2)}, u32[]{:S(2)}) collective-permute-start(bf16[512,1536]{1,0:T(8,128)(2,1)S(1)} %pad_maximum_fusion.2), channel_id=1, source_target_pairs={{0,2},{1,3},{2,0},{3,1},{4,6},{5,7},{6,4},{7,5},{8,10},{9,11},{10,... | collective-permute-start | bytes 4718600 | tf_op jit(solution)/shard_map/ppermute | solution.py:151
  180.5 62.7 %collective-permute-start.13 = (bf16[512,1536]{1,0:T(8,128)(2,1)S(1)}, bf16[512,1536]{1,0:T(8,128)(2,1)S(1)}, u32[]{:S(2)}, u32[]{:S(2)}) collective-permute-start(bf16[512,1536]{1,0:T(8,128)(2,1)S(1)} %pad_maximum_fusion.3), channel_id=1, source_target_pairs={{0,4},{1,5},{2,6},{3,7},{4,0},{5,1},{6,2},{7,3},{8,12},{9,13},{10,... | collective-permute-start | bytes 4718600 | tf_op jit(solution)/shard_map/ppermute | solution.py:151
  260.8 16.4 %collective-permute-start.14 = (bf16[1536,1792]{1,0:T(8,128)(2,1)}, bf16[1536,1792]{1,0:T(8,128)(2,1)}, u32[]{:S(2)}, u32[]{:S(2)}) collective-permute-start(bf16[1536,1792]{1,0:T(8,128)(2,1)} %shard_map.443.refs_4_), channel_id=1, source_target_pairs={{0,1},{1,0},{2,3},{3,2},{4,5},{5,4},{6,7},{7,6},{8,9},{9,8},{10,11... | collective-permute-start | bytes 16515080 | tf_op jit(solution)/shard_map/ppermute | solution.py:104
  261.8 18.9 %collective-permute-start.15 = (bf16[128,1536]{1,0:T(8,128)(2,1)S(1)}, bf16[128,1536]{1,0:T(8,128)(2,1)S(1)}, u32[]{:S(2)}, u32[]{:S(2)}) collective-permute-start(bf16[128,1536]{1,0:T(8,128)(2,1)S(1)} %copy-done.13), channel_id=1, source_target_pairs={{0,1},{1,0},{2,3},{3,2},{4,5},{5,4},{6,7},{7,6},{8,9},{9,8},{10,11... | collective-permute-start | bytes 1179656 | tf_op jit(solution)/shard_map/ppermute | solution.py:104
  376.3 22.0 %collective-permute-start.16 = (bf16[2,128,1664]{2,1,0:T(8,128)(2,1)S(1)}, bf16[2,128,1664]{2,1,0:T(8,128)(2,1)S(1)}, u32[]{:S(2)}, u32[]{:S(2)}) collective-permute-start(bf16[2,128,1664]{2,1,0:T(8,128)(2,1)S(1)} %get-tuple-element.178), channel_id=1, source_target_pairs={{0,2},{1,3},{2,0},{3,1},{4,6},{5,7},{6,4},{7,5},{8,10},{9,11},{10,... | collective-permute-start | bytes 2555912 | tf_op jit(solution)/shard_map/ppermute | solution.py:151
  377.8 21.9 %collective-permute-start.17 = (bf16[2,128,1664]{2,1,0:T(8,128)(2,1)S(1)}, bf16[2,128,1664]{2,1,0:T(8,128)(2,1)S(1)}, u32[]{:S(2)}, u32[]{:S(2)}) collective-permute-start(bf16[2,128,1664]{2,1,0:T(8,128)(2,1)S(1)} %get-tuple-element.177), channel_id=1, source_target_pairs={{0,4},{1,5},{2,6},{3,7},{4,0},{5,1},{6,2},{7,3},{8,12},{9,13},{10,... | collective-permute-start | bytes 2555912 | tf_op jit(solution)/shard_map/ppermute | solution.py:151
  378.5 47.3 %collective-permute-start.18 = (bf16[2,128,1664]{2,1,0:T(8,128)(2,1)S(1)}, bf16[2,128,1664]{2,1,0:T(8,128)(2,1)S(1)}, u32[]{:S(2)}, u32[]{:S(2)}) collective-permute-start(bf16[2,128,1664]{2,1,0:T(8,128)(2,1)S(1)} %get-tuple-element.173), channel_id=1, source_target_pairs={{0,2},{1,3},{2,0},{3,1},{4,6},{5,7},{6,4},{7,5},{8,10},{9,11},{10,... | collective-permute-start | bytes 2555912 | tf_op jit(solution)/shard_map/ppermute | solution.py:151
  379.0 46.8 %collective-permute-start.20 = (bf16[2,128,1664]{2,1,0:T(8,128)(2,1)S(1)}, bf16[2,128,1664]{2,1,0:T(8,128)(2,1)S(1)}, u32[]{:S(2)}, u32[]{:S(2)}) collective-permute-start(bf16[2,128,1664]{2,1,0:T(8,128)(2,1)S(1)} %get-tuple-element.174), channel_id=1, source_target_pairs={{0,4},{1,5},{2,6},{3,7},{4,0},{5,1},{6,2},{7,3},{8,12},{9,13},{10,... | collective-permute-start | bytes 2555912 | tf_op jit(solution)/shard_map/ppermute | solution.py:151
  427.0 15.6 %collective-permute-start.19 = (bf16[1,256,1664]{2,1,0:T(8,128)(2,1)S(1)}, bf16[1,256,1664]{2,1,0:T(8,128)(2,1)}, u32[]{:S(2)}, u32[]{:S(2)}) collective-permute-start(bf16[1,256,1664]{2,1,0:T(8,128)(2,1)S(1)} %fusion.69), channel_id=1, source_target_pairs={{0,4},{1,5},{2,6},{3,7},{4,0},{5,1},{6,2},{7,3},{8,12},{9,13},{10,... | collective-permute-start | bytes 2555912 | tf_op jit(solution)/shard_map/ppermute | solution.py:151
  427.7 16.4 %collective-permute-start.21 = (bf16[1,256,1664]{2,1,0:T(8,128)(2,1)S(1)}, bf16[1,256,1664]{2,1,0:T(8,128)(2,1)}, u32[]{:S(2)}, u32[]{:S(2)}) collective-permute-start(bf16[1,256,1664]{2,1,0:T(8,128)(2,1)S(1)} %fusion.68), channel_id=1, source_target_pairs={{0,2},{1,3},{2,0},{3,1},{4,6},{5,7},{6,4},{7,5},{8,10},{9,11},{10,... | collective-permute-start | bytes 2555912 | tf_op jit(solution)/shard_map/ppermute | solution.py:151
  428.2 50.5 %collective-permute-start.25 = (bf16[1536,1280]{1,0:T(8,128)(2,1)}, bf16[1536,1280]{1,0:T(8,128)(2,1)}, u32[]{:S(2)}, u32[]{:S(2)}) collective-permute-start(bf16[1536,1280]{1,0:T(8,128)(2,1)} %convolution_convert_fusion.2), channel_id=1, source_target_pairs={{0,1},{1,0},{2,3},{3,2},{4,5},{5,4},{6,7},{7,6},{8,9},{9,8},{10,11... | collective-permute-start | bytes 11796488 | tf_op jit(solution)/shard_map/ppermute | solution.py:104
  454.2 24.5 %collective-permute-start.26 = (bf16[640,1536]{1,0:T(8,128)(2,1)}, bf16[640,1536]{1,0:T(8,128)(2,1)S(1)}, u32[]{:S(2)}, u32[]{:S(2)}) collective-permute-start(bf16[640,1536]{1,0:T(8,128)(2,1)} %convolution_convert_fusion.6), channel_id=1, source_target_pairs={{0,1},{1,0},{2,3},{3,2},{4,5},{5,4},{6,7},{7,6},{8,9},{9,8},{10,11... | collective-permute-start | bytes 5898248 | tf_op jit(solution)/shard_map/ppermute | solution.py:104
  489.4 72.0 %all-to-all-start.1 = ((bf16[8,192,1024]{2,1,0:T(8,128)(2,1)}), bf16[8,192,1024]{2,1,0:T(8,128)(2,1)S(1)}, u32[]{:S(2)}, u32[]{:S(2)}) async-start(bf16[8,192,1024]{2,1,0:T(8,128)(2,1)} %shard_map.452), calls=%async_computation.1 | async-start | bytes 6291456 | tf_op jit(solution)/shard_map/all_to_all | solution.py:334
  501.5 18.2 %collective-permute-start.27 = (bf16[1536,768]{1,0:T(8,128)(2,1)}, bf16[1536,768]{1,0:T(8,128)(2,1)}, u32[]{:S(2)}, u32[]{:S(2)}) collective-permute-start(bf16[1536,768]{1,0:T(8,128)(2,1)} %convolution_convert_fusion.5), channel_id=1, source_target_pairs={{0,1},{1,0},{2,3},{3,2},{4,5},{5,4},{6,7},{7,6},{8,9},{9,8},{10,11... | collective-permute-start | bytes 7077896 | tf_op jit(solution)/shard_map/ppermute | solution.py:104
  525.1 16.5 %collective-permute-start.28 = (bf16[2,384,768]{2,1,0:T(8,128)(2,1)}, bf16[2,384,768]{2,1,0:T(8,128)(2,1)}, u32[]{:S(2)}, u32[]{:S(2)}) collective-permute-start(bf16[2,384,768]{2,1,0:T(8,128)(2,1)} %bitcast.51), channel_id=1, source_target_pairs={{0,2},{1,5},{2,0},{3,7},{4,6},{5,1},{6,4},{7,3},{8,10},{9,13},{10,... | collective-permute-start | bytes 3538952 | tf_op jit(solution)/shard_map/ppermute | solution.py:151
  579.1 27.1 %collective-permute-start.31 = (bf16[2,384,1408]{2,1,0:T(8,128)(2,1)}, bf16[2,384,1408]{2,1,0:T(8,128)(2,1)}, u32[]{:S(2)}, u32[]{:S(2)}) collective-permute-start(bf16[2,384,1408]{2,1,0:T(8,128)(2,1)} %bitcast.55), channel_id=1, source_target_pairs={{0,2},{1,5},{2,0},{3,7},{4,6},{5,1},{6,4},{7,3},{8,10},{9,13},{10,... | collective-permute-start | bytes 6488072 | tf_op jit(solution)/shard_map/ppermute | solution.py:151
  580.8 65.2 %all-to-all-start.2 = ((bf16[8,192,768]{2,1,0:T(8,128)(2,1)}), bf16[8,192,768]{2,1,0:T(8,128)(2,1)S(1)}, u32[]{:S(2)}, u32[]{:S(2)}) async-start(bf16[8,192,768]{2,1,0:T(8,128)(2,1)} %shard_map.455), calls=%async_computation.2 | async-start | bytes 4718592 | tf_op jit(solution)/shard_map/all_to_all | solution.py:334
  611.4 30.8 %collective-permute-start.39 = (bf16[384,1408]{1,0:T(8,128)(2,1)}, bf16[384,1408]{1,0:T(8,128)(2,1)}, u32[]{:S(2)}, u32[]{:S(2)}) collective-permute-start(bf16[384,1408]{1,0:T(8,128)(2,1)} %slice_bitcast_fusion.1), channel_id=1, source_target_pairs={{0,4},{1,3},{2,6},{3,1},{4,0},{5,7},{6,2},{7,5},{8,12},{9,11},{10,... | collective-permute-start | bytes 3244040 | tf_op jit(solution)/shard_map/ppermute | solution.py:151
  619.3 76.5 %collective-permute-start.32 = (bf16[2,256,1536]{2,1,0:T(8,128)(2,1)}, bf16[2,256,1536]{2,1,0:T(8,128)(2,1)}, u32[]{:S(2)}, u32[]{:S(2)}) collective-permute-start(bf16[2,256,1536]{2,1,0:T(8,128)(2,1)} %bitcast.57), channel_id=1, source_target_pairs={{0,2},{1,3},{2,0},{3,1},{4,6},{5,7},{6,4},{7,5},{8,10},{9,11},{10,... | collective-permute-start | bytes 4718600 | tf_op jit(solution)/shard_map/ppermute | solution.py:151
  649.2 43.3 %collective-permute-start.40 = (bf16[96,2176]{1,0:T(8,128)(2,1)}, bf16[96,2176]{1,0:T(8,128)(2,1)}, u32[]{:S(2)}, u32[]{:S(2)}) collective-permute-start(bf16[96,2176]{1,0:T(8,128)(2,1)} %slice.569), channel_id=1, source_target_pairs={{0,16},{1,17},{2,18},{3,19},{4,20},{5,21},{6,22},{7,23},{8,0},{9,1... | collective-permute-start | bytes 1253384 | tf_op jit(solution)/shard_map/ppermute | solution.py:151
  669.1 42.0 %collective-permute-start.34 = (bf16[2,256,1536]{2,1,0:T(8,128)(2,1)S(1)}, bf16[2,256,1536]{2,1,0:T(8,128)(2,1)S(1)}, u32[]{:S(2)}, u32[]{:S(2)}) collective-permute-start(bf16[2,256,1536]{2,1,0:T(8,128)(2,1)S(1)} %bitcast.199), channel_id=1, source_target_pairs={{0,4},{1,5},{2,6},{3,7},{4,0},{5,1},{6,2},{7,3},{8,12},{9,13},{10,... | collective-permute-start | bytes 4718600 | tf_op jit(solution)/shard_map/ppermute | solution.py:151
  697.6 32.8 %collective-permute-start.33 = (bf16[1,256,1536]{2,1,0:T(8,128)(2,1)S(1)}, bf16[1,256,1536]{2,1,0:T(8,128)(2,1)S(1)}, u32[]{:S(2)}, u32[]{:S(2)}) collective-permute-start(bf16[1,256,1536]{2,1,0:T(8,128)(2,1)S(1)} %slice.553), channel_id=1, source_target_pairs={{0,4},{1,5},{2,6},{3,7},{4,0},{5,1},{6,2},{7,3},{8,12},{9,13},{10,... | collective-permute-start | bytes 2359304 | tf_op jit(solution)/shard_map/ppermute | solution.py:151
  711.6 19.7 %collective-permute-start.35 = (bf16[1,256,1536]{2,1,0:T(8,128)(2,1)S(1)}, bf16[1,256,1536]{2,1,0:T(8,128)(2,1)S(1)}, u32[]{:S(2)}, u32[]{:S(2)}) collective-permute-start(bf16[1,256,1536]{2,1,0:T(8,128)(2,1)S(1)} %slice.558), channel_id=1, source_target_pairs={{0,2},{1,3},{2,0},{3,1},{4,6},{5,7},{6,4},{7,5},{8,10},{9,11},{10,... | collective-permute-start | bytes 2359304 | tf_op jit(solution)/shard_map/ppermute | solution.py:151
  (157 other events, 1390.5 us)
Sparse Core Ops, SparseCore 0:
  11.6 96.6 all-gather.2
  139.4 171.4 all-gather.4
